TPU v7x, 256 devices: a whole 4x4x8 slice. The times are simulated.
256 devices in a mesh: lev: 8 (over x, core), wave: 32 (over z, y).
Axes of the slice: x: 4, y: 4, z: 8, core: 2. Of those that a mesh axis runs over, the one named last changes fastest.
Arguments:
- grid: bfloat16 [64, 4, 256, 2816], P('lev', None, 'wave'), may hold values from -6 to 6
- halo_values: float32 [32, 32, 64, 4, 128], P('wave', None, 'lev'), may hold values from -6 to 6
- halo_owner: int32 [32, 32], P('wave'), may hold values from 0 to 31, as said below
- halo_block: int32 [32, 32], P('wave'), may hold values from 0 to 175
- halo_count: int32 [32], P('wave'), may hold values from 0 to 32
- wave_list: int32 [1280], replicated, may hold values from 0 to 1279, each once
- legendre: bfloat16 [1280, 256, 1280], P(('lev', 'wave')), may hold values from -0.375 to 0.375
- modes: float32 [64, 64], replicated, may hold values from -0.75 to 0.75
- back: float32 [64, 64], replicated, may hold values from -0.75 to 0.75
- eigen: float32 [64], replicated, may hold values from 0.5 to 50
Outputs:
- spectral: bfloat16 [1280, 64, 4, 2, 1280], P(('lev', 'wave'))
Inputs may be any that keep to these rules, and one draw needn't show every extreme that they name: `halo_owner`: for live slots of band w the owner differs from w by 1 to 2; at most 8 live slots of one band name one owner, and some band sends exactly 8 to each of its 4 neighbours; slots past the count hold arbitrary owners. `wave_list`: each wavenumber once.
All inputs are finite; a program needn't handle non-finite values.
Results may differ from a plain program's by a relative error of at most 0.006.
Values may be sent and summed in bfloat16 or wider, within the bound.
No kernel may reach another device: no remote copies, remote signals or barrier semaphores. Data moves between devices by JAX's collectives and lax.ppermute only.
A program may use at most 128 MiB of HBM per device.

v0:
```python
import math

import jax
import jax.numpy as jnp
from jax import lax
from jax.sharding import PartitionSpec as P

MW = 1280
NLON = 2816
F = 4
BLK = 128
CAP = 8
REACH = 2


def passed_along(block, axis, distance):
    devices = range(lax.axis_size(axis))
    route = [(i - distance, i) for i in devices if i - distance in devices]
    return lax.ppermute(block, axis, route)


def dft_table(wave_list, width):
    longitude = jnp.arange(width, dtype=jnp.int32)
    phase = longitude[:, None] * wave_list[None, :] % width
    angle = phase.astype(jnp.float32) * (2.0 * math.pi / width)
    scale = 1.0 / math.sqrt(width)
    return jnp.stack([jnp.cos(angle) * scale, -jnp.sin(angle) * scale], 1).astype(jnp.bfloat16)


def vertical(coefficient, modes, back, eigen, total):
    order = jnp.arange(total, dtype=jnp.float32)
    ratio = order * (order + 1.0) / (total * (total - 1.0))
    projected = jnp.einsum("skfcn,ki->sifcn", coefficient, modes, precision=lax.Precision.HIGHEST)
    scaled = projected / (1.0 + eigen[None, :, None, None, None] * ratio[None, None, None, None, :])
    return jnp.einsum("sifcn,ik->skfcn", scaled, back, precision=lax.Precision.HIGHEST)


def bucket_slots(target, buckets, live, flat_values, block_float):
    matches = (
        (target[:, None] == jnp.arange(buckets, dtype=jnp.int32)[None, :]) & live[:, None]
    ).astype(jnp.int32)
    before = jnp.cumsum(matches, 0) - matches
    position = jnp.sum(matches * before, 1)
    index = target * CAP + position
    place = (
        (index[None, :] == jnp.arange(buckets * CAP, dtype=jnp.int32)[:, None]) & live[None, :]
    ).astype(jnp.float32)
    packed = jnp.dot(place, flat_values, precision=lax.Precision.HIGHEST)
    blocks = jnp.dot(place, block_float, precision=lax.Precision.HIGHEST)
    return (packed, blocks)


def shards(
    grid, halo_values, halo_owner, halo_block, halo_count, wave_list, legendre, modes, back, eigen
):
    bands = lax.axis_size("wave")
    my_band = lax.axis_index("wave")
    lev_dev = grid.shape[0]
    lat_dev = grid.shape[2]
    slots = halo_values.shape[1]
    row_width = lev_dev * F * BLK
    live = jnp.arange(slots, dtype=jnp.int32) < halo_count[0]
    flat_values = halo_values[0].reshape(slots, row_width)
    block_float = halo_block[0].astype(jnp.float32)
    owner = halo_owner[0]
    offset = owner - my_band
    target = jnp.where(offset < 0, offset + REACH, offset + REACH - 1)
    packed, blocks = bucket_slots(target, 2 * REACH, live, flat_values, block_float)
    offsets = list(range(-REACH, 0)) + list(range(1, REACH + 1))
    value_parts = []
    block_parts = []
    for number, step in enumerate(offsets):
        sent_values = packed[number * CAP : (number + 1) * CAP]
        sent_blocks = blocks[number * CAP : (number + 1) * CAP]
        came_values, came_blocks = passed_along((sent_values, sent_blocks), "wave", step)
        value_parts.append(came_values)
        block_parts.append(came_blocks)
    got_values = jnp.concatenate(value_parts, 0)
    got_blocks = jnp.concatenate(block_parts, 0)
    nblk = lat_dev * NLON // BLK
    landing = (
        got_blocks.astype(jnp.int32)[:, None] == jnp.arange(nblk, dtype=jnp.int32)[None, :]
    ).astype(jnp.float32)
    summed = jnp.einsum("rb,rm->bm", landing, got_values, precision=lax.Precision.HIGHEST)
    summed = summed.reshape(lat_dev, NLON // BLK, lev_dev, F, BLK)
    contribution = jnp.transpose(summed, (2, 3, 0, 1, 4)).reshape(lev_dev, F, lat_dev, NLON)
    surface = (grid.astype(jnp.float32) + contribution).astype(jnp.bfloat16)
    table = dft_table(wave_list, NLON)
    fourier = jnp.einsum(
        "kfjx,xcs->sjkfc", surface, table, preferred_element_type=jnp.float32
    ).astype(jnp.bfloat16)
    fourier = fourier.reshape(MW, lat_dev, lev_dev * F * 2)
    moved = lax.all_to_all(fourier, "lev", split_axis=0, concat_axis=2, tiled=True)
    moved = lax.all_to_all(moved, "wave", split_axis=0, concat_axis=1, tiled=True)
    slot_dev = legendre.shape[0]
    first_slot = (lax.axis_index("lev") * bands + my_band) * slot_dev
    numbers = lax.dynamic_slice_in_dim(wave_list, first_slot, slot_dev, 0)
    coefficient = jnp.einsum("sjm,sjn->smn", moved, legendre, preferred_element_type=jnp.float32)
    levels = moved.shape[2] // (F * 2)
    coefficient = coefficient.reshape(slot_dev, levels, F, 2, MW)
    order = jnp.arange(MW, dtype=jnp.int32)
    keep = (order[None, :] >= numbers[:, None]).astype(jnp.float32)
    coefficient = coefficient * keep[:, None, None, None, :]
    return vertical(coefficient, modes, back, eigen, MW).astype(jnp.bfloat16)


def solution(mesh):
    placed = (
        P("lev", None, "wave", None),
        P("wave", None, "lev", None, None),
        P("wave", None),
        P("wave", None),
        P("wave"),
        P(),
        P(("lev", "wave"), None, None),
        P(),
        P(),
        P(),
    )
    return jax.shard_map(
        shards,
        mesh=mesh,
        in_specs=placed,
        out_specs=P(("lev", "wave"), None, None, None, None),
        check_vma=False,
    )
```

profile of v0, /device:TPU:1, one launch (start us, length us, event | category | flops | bytes accessed | tf_op | source)
XLA Modules:
  0.0 291.5 jit_solution(15828466299352861047)
XLA Ops:
  0.0 0.0 copy-start
  0.8 0.8 fusion.50
  1.7 0.1 fusion.33
  1.7 0.1 reduce_window_sum.11
  1.8 0.2 select_reduce_fusion
  2.0 0.7 fusion.43
  2.6 0.8 convolution_bitcast_fusion
  3.4 0.1 fusion.47
  3.5 1.3 collective-permute-start
  4.8 2.1 reshape_squeeze.3
  6.9 1.4 fusion.35
  8.3 1.3 collective-permute-start.4
  9.6 1.3 collective-permute-start.5
  10.9 4.7 %collective-permute-start.6 = (f32[8,4096]{1,0:T(8,128)S(1)}, f32[8,4096]{1,0:T(8,128)S(1)}, u32[]{:S(2)}, u32[]{:S(2)}) collective-permute-start(f32[8,4096]{1,0:T(8,128)S(1)} %get-tuple-element.7), channel_id=1, source_target_pairs={{0,1},{1,2},{2,3},{3,4},{4,5},{5,6},{6,7},{7,8},{8,9},{9,10},{10,1... | collective-permute-start | bytes 393224 | tf_op jit(solution)/shard_map/ppermute | solution.py:19
  15.6 6.7 %collective-permute-start.7 = (f32[8,4096]{1,0:T(8,128)S(1)}, f32[8,4096]{1,0:T(8,128)S(1)}, u32[]{:S(2)}, u32[]{:S(2)}) collective-permute-start(f32[8,4096]{1,0:T(8,128)S(1)} %get-tuple-element.6), channel_id=1, source_target_pairs={{0,2},{1,3},{2,4},{3,5},{4,6},{5,7},{6,8},{7,9},{8,10},{9,11},{10,... | collective-permute-start | bytes 393224 | tf_op jit(solution)/shard_map/ppermute | solution.py:19
  22.3 63.7 %multiply_convert_fusion.1 = (bf16[2816,1,1280]{2,0,1:T(8,128)(2,1)}, bf16[2816,1,1280]{2,0,1:T(8,128)(2,1)}) fusion(s32[1280]{0:T(1024)} %param.15), kind=kLoop, calls=%fused_computation.8 | loop fusion | flops 50462720 | bytes 14423040 | tf_op jit(solution)/shard_map/convert
  86.0 0.0 collective-permute-done
  86.0 1.3 collective-permute-start.1
  87.3 4.5 %collective-permute-done.1 = f32[8]{0:T(128)S(1)} collective-permute-done((f32[8]{0:T(128)S(1)}, f32[8]{0:T(128)S(1)}, u32[]{:S(2)}, u32[]{:S(2)}) %collective-permute-start.1) | collective-permute-done | bytes 64 | tf_op jit(solution)/shard_map/ppermute | solution.py:19
  91.8 3.3 %collective-permute-start.2 = (f32[8]{0:T(128)S(1)}, f32[8]{0:T(128)S(1)}, u32[]{:S(2)}, u32[]{:S(2)}) collective-permute-start(f32[8]{0:T(128)S(1)} %get-tuple-element.13), channel_id=1, source_target_pairs={{0,1},{1,2},{2,3},{3,4},{4,5},{5,6},{6,7},{7,8},{8,9},{9,10},{10,1... | collective-permute-start | bytes 104 | tf_op jit(solution)/shard_map/ppermute | solution.py:19
  95.1 0.7 collective-permute-done.2
  95.8 6.4 %collective-permute-start.3 = (f32[8]{0:T(128)S(1)}, f32[8]{0:T(128)S(1)}, u32[]{:S(2)}, u32[]{:S(2)}) collective-permute-start(f32[8]{0:T(128)S(1)} %get-tuple-element.12), channel_id=1, source_target_pairs={{0,2},{1,3},{2,4},{3,5},{4,6},{5,7},{6,8},{7,9},{8,10},{9,11},{10,... | collective-permute-start | bytes 104 | tf_op jit(solution)/shard_map/ppermute | solution.py:19
  102.2 0.7 collective-permute-done.3
  102.9 0.1 maximum_convert_fusion
  103.0 0.0 collective-permute-done.4
  103.0 0.0 collective-permute-done.5
  103.0 0.0 collective-permute-done.6
  103.0 0.0 collective-permute-done.7
  103.0 3.0 %fusion.20 = f32[176,4096]{1,0:T(8,128)} fusion(f32[8,4096]{1,0:T(8,128)S(1)} %collective-permute-done.7, f32[8,4096]{1,0:T(8,128)S(1)} %collective-permute-done.6, f32[8,4096]{1,0:T(8,128)S(1)} %collective-permute-done.5, f32[8,4096]{1,0:T(8,128)S(1)} %collective-permute-done.4, s32[32]{0:T(128)S(1)} %maximum_convert_fusion), kind=kOutput, calls=%fused_computation.30 | convolution fusion | flops 277222912 | bytes 3408000 | tf_op jit(solution)/shard_map/rb,rm->bm/dot_general | solution.py:84
  106.0 4.9 %reshape.213 = f32[8,22,8,4,128]{4,3,2,1,0:T(4,128)} reshape(f32[176,4096]{1,0:T(8,128)} %fusion.20) | data formatting | bytes 5767168 | tf_op jit(solution)/shard_map/reshape | solution.py:85
  110.9 10.5 %fusion.14 = bf16[1280,8,8,4,2]{0,1,3,2,4:T(8,128)(2,1)S(1)} fusion(bf16[2816,1,1280]{2,0,1:T(8,128)(2,1)} %get-tuple-element.10, bf16[2816,1,1280]{2,0,1:T(8,128)(2,1)} %get-tuple-element.9, f32[8,4,8,22,128]{4,1,0,3,2:T(4,128)} %bitcast.69, bf16[8,4,8,2816]{3,2,1,0:T(8,128)(2,1)} %param.10), kind=kOutput, calls=%fused_computation.23 | convolution fusion | flops 3722641408 | bytes 20054016 | tf_op jit(solution)/shard_map/kfjx,xcs->sjkfc/dot_general | solution.py:89
  121.4 1.2 copy.32
  122.6 5.1 %copy.33 = bf16[1280,8,64]{2,1,0:T(8,128)(2,1)} copy(bf16[1280,8,64]{0,1,2:T(8,128)(2,1)} %bitcast.68) | data formatting | bytes 2621440 | tf_op jit(solution)/shard_map/reshape | solution.py:92
  127.7 4.7 %reshape.223 = bf16[8,2,40960]{2,1,0:T(2,128)(2,1)} reshape(bf16[1280,8,64]{2,1,0:T(8,128)(2,1)} %copy.33) | data formatting | bytes 2621440
  132.4 27.3 %all_to_all.36 = bf16[8,2,40960]{2,1,0:T(2,128)(2,1)} all-to-all(bf16[8,2,40960]{2,1,0:T(2,128)(2,1)} %reshape.223), channel_id=1, replica_groups=mesh['lev'=8,'wave'=32] {'lev'}, dimensions={0} | all-to-all | bytes 2621440 | tf_op jit(solution)/shard_map/all_to_all | solution.py:93
  159.6 0.0 copy-start.3
  159.6 4.6 %reshape.224 = bf16[1280,8,64]{2,1,0:T(8,128)(2,1)} reshape(bf16[8,2,40960]{2,1,0:T(2,128)(2,1)} %all_to_all.36) | data formatting | bytes 2621440
  164.2 6.3 %copy.58 = bf16[8,160,8,64]{3,0,2,1:T(8,128)(2,1)} copy(bf16[8,160,8,64]{3,2,1,0:T(8,128)(2,1)} %bitcast.66) | data formatting | bytes 2621440 | tf_op jit(solution)/shard_map/all_to_all | solution.py:93
  170.5 4.5 %all_to_all.29 = bf16[160,8,512]{2,1,0:T(8,128)(2,1)} reshape(bf16[160,8,8,64]{3,2,1,0:T(8,128)(2,1)} %bitcast.67) | data formatting | bytes 2621440 | tf_op jit(solution)/shard_map/all_to_all | solution.py:93
  175.0 15.3 %all-to-all-start.1 = ((bf16[160,8,512]{2,1,0:T(8,128)(2,1)}), bf16[160,8,512]{2,1,0:T(8,128)(2,1)}, u32[]{:S(2)}, u32[]{:S(2)}) async-start(bf16[160,8,512]{2,1,0:T(8,128)(2,1)} %all_to_all.29), calls=%async_computation.1 | async-start | bytes 2621440 | tf_op jit(solution)/shard_map/all_to_all | solution.py:94
  190.3 0.8 dynamic_slice.3
  191.1 0.1 fusion.28
  191.2 0.0 copy-done.3
  191.2 0.8 multiply_add_fusion
  192.0 29.3 %all-to-all-done.1 = bf16[160,8,512]{2,1,0:T(8,128)(2,1)} async-done(((bf16[160,8,512]{2,1,0:T(8,128)(2,1)}), bf16[160,8,512]{2,1,0:T(8,128)(2,1)}, u32[]{:S(2)}, u32[]{:S(2)}) %all-to-all-start.1) | async-done | bytes 1310752 | tf_op jit(solution)/shard_map/all_to_all | solution.py:94
  221.3 0.0 copy-done
  221.3 7.9 %fusion.17 = f32[5,512,1280]{2,1,0:T(8,128)} fusion(bf16[5,256,1280]{2,1,0:T(8,128)(2,1)S(1)} %copy-done, bf16[5,32,8,512]{3,2,0,1:T(8,128)(2,1)} %bitcast.17), kind=kOutput, calls=%fused_computation.26 | convolution fusion | flops 1677721600 | bytes 17694720 | tf_op jit(solution)/shard_map/sjm,sjn->smn/dot_general | solution.py:98
  229.2 0.0 copy-start.2
  229.2 15.7 %reshape.216 = f32[5,64,4,2,1280]{4,3,2,1,0:T(2,128)} reshape(f32[5,512,1280]{2,1,0:T(8,128)} %fusion.17) | data formatting | bytes 26214400 | tf_op jit(solution)/shard_map/reshape | solution.py:100
  244.9 0.0 copy-done.2
  244.9 0.0 copy-start.1
  244.9 0.0 copy-start.4
  244.9 19.1 %fusion.9 = f32[5,4,2,1280,64]{3,4,2,1,0:T(8,128)S(1)} fusion(f32[5,64,4,2,1280]{4,3,2,1,0:T(2,128)} %reshape.216, f32[5,1280]{1,0:T(8,128)S(1)} %fusion.28, f32[64,64]{1,0:T(8,128)S(1)} %copy-done.2), kind=kOutput, calls=%fused_computation.16 | convolution fusion | flops 2519859200 | bytes 26256384 | tf_op jit(solution)/shard_map/skfcn,ki->sifcn/dot_general | solution.py:33
  264.0 0.0 copy-done.1
  264.0 0.0 copy-done.4
  264.0 13.2 %convert_bitcast_fusion = bf16[5,64,4,2,1280]{4,1,3,2,0:T(8,128)(2,1)S(1)} fusion(f32[5,4,2,1280,64]{3,4,2,1,0:T(8,128)S(1)} %fusion.9, f32[64,1280]{1,0:T(8,128)S(1)} %copy-done.1, f32[64,64]{1,0:T(8,128)S(1)} %copy-done.4), kind=kOutput, calls=%fused_computation.17 | convolution fusion | flops 2523136000 | bytes 20004864 | tf_op jit(solution)/shard_map/sifcn,ik->skfcn/dot_general | solution.py:35
  277.2 14.3 %copy.40 = bf16[5,64,4,2,1280]{4,3,2,1,0:T(2,128)(2,1)} copy(bf16[5,64,4,2,1280]{4,1,3,2,0:T(8,128)(2,1)S(1)} %convert_bitcast_fusion) | data formatting | bytes 13107200 | tf_op jit(solution)/shard_map/convert_element_type | solution.py:104
  (3 shorter events, 0.1 us)
Async XLA Ops:
  0.0 221.3 %copy-start = (bf16[5,256,1280]{2,1,0:T(8,128)(2,1)S(1)}, bf16[5,256,1280]{2,1,0:T(8,128)(2,1)}, u32[]{:S(2)}) copy-start(bf16[5,256,1280]{2,1,0:T(8,128)(2,1)} %param.16) | copy-start | bytes 9830404
  3.5 82.5 %collective-permute-start = (f32[8]{0:T(128)S(1)}, f32[8]{0:T(128)S(1)}, u32[]{:S(2)}, u32[]{:S(2)}) collective-permute-start(f32[8]{0:T(128)S(1)} %get-tuple-element.11), channel_id=1, source_target_pairs={{2,0},{3,1},{4,2},{5,3},{6,4},{7,5},{8,6},{9,7},{10,8},{11,9},{12,... | collective-permute-start | bytes 104 | tf_op jit(solution)/shard_map/ppermute | solution.py:19
  8.3 94.7 %collective-permute-start.4 = (f32[8,4096]{1,0:T(8,128)S(1)}, f32[8,4096]{1,0:T(8,128)S(1)}, u32[]{:S(2)}, u32[]{:S(2)}) collective-permute-start(f32[8,4096]{1,0:T(8,128)S(1)} %get-tuple-element.5), channel_id=1, source_target_pairs={{2,0},{3,1},{4,2},{5,3},{6,4},{7,5},{8,6},{9,7},{10,8},{11,9},{12,... | collective-permute-start | bytes 393224 | tf_op jit(solution)/shard_map/ppermute | solution.py:19
  9.6 93.4 %collective-permute-start.5 = (f32[8,4096]{1,0:T(8,128)S(1)}, f32[8,4096]{1,0:T(8,128)S(1)}, u32[]{:S(2)}, u32[]{:S(2)}) collective-permute-start(f32[8,4096]{1,0:T(8,128)S(1)} %get-tuple-element.8), channel_id=1, source_target_pairs={{1,0},{2,1},{3,2},{4,3},{5,4},{6,5},{7,6},{8,7},{9,8},{10,9},{11,1... | collective-permute-start | bytes 393224 | tf_op jit(solution)/shard_map/ppermute | solution.py:19
  10.9 92.1 %collective-permute-start.6 = (f32[8,4096]{1,0:T(8,128)S(1)}, f32[8,4096]{1,0:T(8,128)S(1)}, u32[]{:S(2)}, u32[]{:S(2)}) collective-permute-start(f32[8,4096]{1,0:T(8,128)S(1)} %get-tuple-element.7), channel_id=1, source_target_pairs={{0,1},{1,2},{2,3},{3,4},{4,5},{5,6},{6,7},{7,8},{8,9},{9,10},{10,1... | collective-permute-start | bytes 393224 | tf_op jit(solution)/shard_map/ppermute | solution.py:19
  15.6 87.4 %collective-permute-start.7 = (f32[8,4096]{1,0:T(8,128)S(1)}, f32[8,4096]{1,0:T(8,128)S(1)}, u32[]{:S(2)}, u32[]{:S(2)}) collective-permute-start(f32[8,4096]{1,0:T(8,128)S(1)} %get-tuple-element.6), channel_id=1, source_target_pairs={{0,2},{1,3},{2,4},{3,5},{4,6},{5,7},{6,8},{7,9},{8,10},{9,11},{10,... | collective-permute-start | bytes 393224 | tf_op jit(solution)/shard_map/ppermute | solution.py:19
  86.0 5.8 %collective-permute-start.1 = (f32[8]{0:T(128)S(1)}, f32[8]{0:T(128)S(1)}, u32[]{:S(2)}, u32[]{:S(2)}) collective-permute-start(f32[8]{0:T(128)S(1)} %get-tuple-element.14), channel_id=1, source_target_pairs={{1,0},{2,1},{3,2},{4,3},{5,4},{6,5},{7,6},{8,7},{9,8},{10,9},{11,1... | collective-permute-start | bytes 104 | tf_op jit(solution)/shard_map/ppermute | solution.py:19
  91.8 4.1 %collective-permute-start.2 = (f32[8]{0:T(128)S(1)}, f32[8]{0:T(128)S(1)}, u32[]{:S(2)}, u32[]{:S(2)}) collective-permute-start(f32[8]{0:T(128)S(1)} %get-tuple-element.13), channel_id=1, source_target_pairs={{0,1},{1,2},{2,3},{3,4},{4,5},{5,6},{6,7},{7,8},{8,9},{9,10},{10,1... | collective-permute-start | bytes 104 | tf_op jit(solution)/shard_map/ppermute | solution.py:19
  95.8 7.1 %collective-permute-start.3 = (f32[8]{0:T(128)S(1)}, f32[8]{0:T(128)S(1)}, u32[]{:S(2)}, u32[]{:S(2)}) collective-permute-start(f32[8]{0:T(128)S(1)} %get-tuple-element.12), channel_id=1, source_target_pairs={{0,2},{1,3},{2,4},{3,5},{4,6},{5,7},{6,8},{7,9},{8,10},{9,11},{10,... | collective-permute-start | bytes 104 | tf_op jit(solution)/shard_map/ppermute | solution.py:19
  159.6 31.5 %copy-start.3 = (f32[64]{0:T(128)S(1)}, f32[64]{0:T(128)}, u32[]{:S(2)}) copy-start(f32[64]{0:T(128)} %param.19) | copy-start | bytes 772
  175.0 46.3 %all-to-all-start.1 = ((bf16[160,8,512]{2,1,0:T(8,128)(2,1)}), bf16[160,8,512]{2,1,0:T(8,128)(2,1)}, u32[]{:S(2)}, u32[]{:S(2)}) async-start(bf16[160,8,512]{2,1,0:T(8,128)(2,1)} %all_to_all.29), calls=%async_computation.1 | async-start | bytes 2621440 | tf_op jit(solution)/shard_map/all_to_all | solution.py:94
  229.2 15.7 %copy-start.2 = (f32[64,64]{1,0:T(8,128)S(1)}, f32[64,64]{1,0:T(8,128)}, u32[]{:S(2)}) copy-start(f32[64,64]{1,0:T(8,128)} %param.17) | copy-start | bytes 49156
  244.9 19.1 %copy-start.1 = (f32[64,1280]{1,0:T(8,128)S(1)}, f32[64,1280]{1,0:T(8,128)}, u32[]{:S(2)}) copy-start(f32[64,1280]{1,0:T(8,128)} %multiply_add_fusion) | copy-start | bytes 983044
  244.9 19.1 %copy-start.4 = (f32[64,64]{1,0:T(8,128)S(1)}, f32[64,64]{1,0:T(8,128)}, u32[]{:S(2)}) copy-start(f32[64,64]{1,0:T(8,128)} %param.18) | copy-start | bytes 49156
where the time goes:
time: 295 us; the launch traced here: 292 us
  other arithmetic  66.5 us (23%)
  local copies, waits for them, and re-layouts  64.2 us (22%)
  matrix products  55.8 us (19%)
  starting transfers between devices  41.5 us (14%)
  waiting for transfers between devices  35.2 us (12%)
  blocking collectives  27.3 us (9%)
    another operation x1, other arithmetic  63.7 us
    all_to_all x1, waiting for transfers between devices, shards(): lax.all_to_all(moved, 'wave', split_axis=0, concat_axis=1, tiled=True)  29.3 us
    all_to_all x1, blocking collectives, shards(): lax.all_to_all(fourier, 'lev', split_axis=0, concat_axis=2, tiled=True)  27.3 us
    ppermute x8, starting transfers between devices, passed_along(): return lax.ppermute(block, axis, route)  26.3 us
    dot_general x1, matrix products, vertical(): jnp.einsum('skfcn,ki->sifcn', coefficient, modes, precision=lax.Precision...  19.1 us
    reshape x1, local copies, waits for them, and re-layouts, shards(): coefficient = coefficient.reshape(slot_dev, levels, F, 2, MW)  15.7 us
    all_to_all x1, starting transfers between devices, shards(): lax.all_to_all(moved, 'wave', split_axis=0, concat_axis=1, tiled=True)  15.3 us
    convert_element_type x1, local copies, waits for them, and re-layouts, shards(): return vertical(coefficient, modes, back, eigen, MW).astype(jnp.bfloat16)  14.3 us
  transfers between devices with their start and end apart: 9, of which 4 were waited for; matrix products, arithmetic and copies ran while one was open for 24% of the time, Pallas kernels for 0%

commit v1 on v0

v1 whole, which is shorter than its diff:
```python
import functools
import math

import jax
import jax.numpy as jnp
import ml_dtypes
import numpy as np
from jax import lax
from jax.experimental import pallas as pl
from jax.experimental.pallas import tpu as pltpu
from jax.sharding import PartitionSpec as P

MW = 1280
NLON = 2816
F = 4
LEV = 64
BLK = 128
CAP = 8
REACH = 2
SLOTS = 32
NLAT = 256
HALF = NLON // 2
CHUNKS = NLON // BLK
OFFSETS = (-2, -1, 1, 2)
MSG = CAP * 32 + 16
BF = jnp.bfloat16
F32 = jnp.float32

MIB = 1 << 20


def half_table():
    order = np.arange(MW, dtype=np.int64).reshape(MW // 2, 2).T
    phase = order[:, :, None] * np.arange(HALF, dtype=np.int64)[None, None, :] % NLON
    angle = phase.astype(np.float32) * np.float32(2.0 * math.pi / NLON)
    scale = np.float32(1.0 / math.sqrt(NLON))
    both = np.stack([np.cos(angle) * scale, -np.sin(angle) * scale], 1)
    return both.astype(ml_dtypes.bfloat16)


def row_order():
    source = np.arange(640).reshape(4, 8, 5, 2, 2)
    target = source.transpose(2, 3, 1, 4, 0).reshape(640)
    return (target[:, None] == np.arange(640)[None, :]).astype(ml_dtypes.bfloat16)


def dot(a, b):
    return lax.dot_general(a, b, (((1,), (0,)), ((), ())), preferred_element_type=F32)


def dot_nt(a, b):
    return lax.dot_general(a, b, (((1,), (1,)), ((), ())), preferred_element_type=F32)


def pack_kernel(owner, block, count, values, *outs):
    band = lax.axis_index("wave")
    for out in outs:
        out[...] = jnp.zeros((MSG, BLK), BF)
    row = lax.broadcasted_iota(jnp.int32, (16, BLK), 0)
    place = [jnp.int32(0)] * 4
    index = [jnp.zeros((16, BLK), F32)] * 4
    for slot in range(SLOTS):
        step = owner[0, slot] - band
        live = slot < count[0]
        which = block[0, slot].astype(F32)
        for number, offset in enumerate(OFFSETS):
            hit = jnp.logical_and(live, step == offset)
            at = place[number]

            @pl.when(hit)
            def _(out=outs[number], at=at, slot=slot):
                out[pl.ds(pl.multiple_of(at * 32, 32), 32), :] = values[slot].astype(BF)

            mark = jnp.where(hit, at, -1)
            index[number] = jnp.where(row == mark, which, index[number])
            place[number] = at + hit.astype(jnp.int32)
    for out, marks in zip(outs, index):
        out[pl.ds(CAP * 32, 16), :] = marks.astype(BF)


def pack(owner, block, count, values):
    smem = pl.BlockSpec(memory_space=pltpu.SMEM)
    vmem = pl.BlockSpec(memory_space=pltpu.VMEM)
    return pl.pallas_call(
        pack_kernel,
        out_shape=[jax.ShapeDtypeStruct((MSG, BLK), BF)] * 4,
        in_specs=[smem, smem, smem, vmem],
        out_specs=[vmem] * 4,
        compiler_params=pltpu.CompilerParams(vmem_limit_bytes=8 * MIB),
        name="pack",
    )(owner, block, count, values)


def dft_kernel(
    grid, m0, m1, m2, m3, waves, table, out, acc, surf, held, four, strided, marks, marks_s, sem, sem_s
):
    copies = [
        pltpu.make_async_copy(table.at[p], held.at[p], sem.at[p]) for p in range(2)
    ]
    for copy in copies:
        copy.start()
    messages = (m0, m1, m2, m3)
    for number, message in enumerate(messages):
        marks[pl.ds(number * CAP, CAP), :] = (
            message[pl.ds(CAP * 32, 16), :].astype(F32)[:CAP].astype(jnp.int32)
        )
    to_scalar = pltpu.make_async_copy(marks, marks_s, sem_s)
    to_scalar.start()
    for kf in range(32):
        row = grid[kf].astype(F32)
        for c in range(CHUNKS):
            acc[c, pl.ds(kf, 8, stride=32), :] = row[:, c * BLK : (c + 1) * BLK]
    to_scalar.wait()
    for number, message in enumerate(messages):
        for r in range(CAP):
            b = marks_s[number * CAP + r, 0]
            j = b // CHUNKS
            c = b - j * CHUNKS
            at = pl.ds(pl.multiple_of(j * 32, 32), 32)
            acc[c, at, :] = acc[c, at, :] + message[pl.ds(r * 32, 32), :].astype(F32)
    for c in range(CHUNKS // 2):
        near, far = acc[c], acc[c + CHUNKS // 2]
        surf[0, :, c * BLK : (c + 1) * BLK] = (near + far).astype(BF)
        surf[1, :, c * BLK : (c + 1) * BLK] = (near - far).astype(BF)
    half = MW // 2
    for p in range(2):
        copies[p].wait()
        for part in range(2):
            four[p * half : (p + 1) * half, part * 256 : (part + 1) * 256] = dot_nt(
                held[p, part], surf[p]
            ).astype(BF)
    column = lax.broadcasted_iota(jnp.int32, (BLK, BLK), 1)
    for b in range(MW // BLK):
        m = waves[b : b + 1, :]
        key = (m % 2) * half + m // 2
        key = jnp.broadcast_to(key.astype(F32), (BLK, BLK)).T.astype(jnp.int32)
        pick = jnp.concatenate(
            [jnp.where(key == column + t * BLK, 1.0, 0.0).astype(BF) for t in range(MW // BLK)], 1
        )
        rows = dot(pick, four[...])
        for q in range(4):
            strided[pl.ds(q, BLK, stride=4), :] = rows[:, q * BLK : (q + 1) * BLK]
        out[b * 512 : (b + 1) * 512, :] = strided[...].astype(BF)


def dft(grid, messages, waves, table):
    vmem = pl.BlockSpec(memory_space=pltpu.VMEM)
    return pl.pallas_call(
        dft_kernel,
        out_shape=jax.ShapeDtypeStruct((MW * 4, BLK), BF),
        in_specs=[vmem] * 6 + [pl.BlockSpec(memory_space=pl.ANY)],
        out_specs=vmem,
        scratch_shapes=[
            pltpu.VMEM((CHUNKS, 256, BLK), F32),
            pltpu.VMEM((2, 256, HALF), BF),
            pltpu.VMEM((2, 2, MW // 2, HALF), BF),
            pltpu.VMEM((MW, 512), BF),
            pltpu.VMEM((512, BLK), F32),
            pltpu.VMEM((SLOTS, BLK), jnp.int32),
            pltpu.SMEM((SLOTS, BLK), jnp.int32),
            pltpu.SemaphoreType.DMA((2,)),
            pltpu.SemaphoreType.DMA,
        ],
        compiler_params=pltpu.CompilerParams(vmem_limit_bytes=32 * MIB),
        name="dft",
    )(grid, *messages, waves, table)


def prepare_kernel(modes, back, eigen, ahead, behind, scale):
    spread = jnp.where(
        lax.broadcasted_iota(jnp.int32, (256, LEV), 0) // F
        == lax.broadcasted_iota(jnp.int32, (256, LEV), 1),
        1.0,
        0.0,
    )
    picks = spread.astype(BF)
    same = (
        lax.broadcasted_iota(jnp.int32, (256, 256), 0) % F
        == lax.broadcasted_iota(jnp.int32, (256, 256), 1) % F
    )
    for source, target in ((modes, ahead), (back, behind)):
        rows = dot_nt(picks, source[...].astype(BF)).astype(BF)
        whole = dot_nt(rows, picks)
        target[...] = jnp.where(same, whole, 0.0).astype(BF)
    value = jnp.sum(spread * eigen[...], axis=1, keepdims=True)
    order = lax.broadcasted_iota(jnp.int32, (1, MW), 1).astype(F32)
    ratio = order * (order + 1.0) / (MW * (MW - 1.0))
    scale[...] = 1.0 / (1.0 + value * ratio)


def prepare(modes, back, eigen):
    vmem = pl.BlockSpec(memory_space=pltpu.VMEM)
    return pl.pallas_call(
        prepare_kernel,
        out_shape=[
            jax.ShapeDtypeStruct((256, 256), BF),
            jax.ShapeDtypeStruct((256, 256), BF),
            jax.ShapeDtypeStruct((256, MW), F32),
        ],
        in_specs=[vmem] * 3,
        out_specs=[vmem] * 3,
        compiler_params=pltpu.CompilerParams(vmem_limit_bytes=16 * MIB),
        name="prepare",
    )(modes, back, eigen)


def receive_kernel(
    waves, moved, legendre, ahead, behind, scale, order, out, sorted_rows, strided, packed, sems
):
    slot = pl.program_id(0)
    turn = lax.rem(slot, 2)

    def sends(number, turn):
        return [
            pltpu.make_async_copy(
                packed.at[turn, :, t],
                out.at[pl.ds(number * 256, 256), :, pl.ds(t * BLK, BLK)],
                sems.at[turn, t],
            )
            for t in range(MW // BLK)
        ]

    @pl.when(slot == 0)
    def _():
        for g in range(4):
            rows = [moved[lev * 640 + g * 160 : lev * 640 + (g + 1) * 160, :] for lev in range(8)]
            mixed = jnp.concatenate(
                [
                    jnp.concatenate([r[:, j * 32 : (j + 1) * 32] for r in rows], 1)
                    for j in range(4)
                ],
                0,
            )
            natural = dot(order[...], mixed).astype(BF)
            for sc in range(10):
                sorted_rows[sc, g * 64 : (g + 1) * 64, :] = natural[sc * 64 : (sc + 1) * 64]

    first = (lax.axis_index("lev") * 32 + lax.axis_index("wave")) * 5
    number = waves[first + slot]
    keep = lax.broadcasted_iota(jnp.int32, (1, MW), 1) >= number
    for part in range(2):
        projected = dot_nt(ahead[...], sorted_rows[slot * 2 + part]).astype(BF)
        scaled = dot(projected, legendre[0]) * jnp.where(keep, scale[...], 0.0)
        final = dot(behind[...], scaled.astype(BF))
        for t in range(MW // BLK):
            strided[pl.ds(t * 2 + part, 256, stride=20), :] = final[:, t * BLK : (t + 1) * BLK]

    @pl.when(slot >= 2)
    def _():
        for copy in sends(slot - 2, turn):
            copy.wait()

    packed.at[turn].reshape(5120, BLK)[...] = strided[...].astype(BF)
    for copy in sends(slot, turn):
        copy.start()

    @pl.when(slot == 4)
    def _():
        for copy in sends(slot - 1, 1 - turn) + sends(slot, turn):
            copy.wait()


def receive(waves, moved, legendre, ahead, behind, scale, order):
    vmem = pl.BlockSpec(memory_space=pltpu.VMEM)
    return pl.pallas_call(
        receive_kernel,
        grid=(5,),
        out_shape=jax.ShapeDtypeStruct((5 * 256, 2, MW), BF),
        in_specs=[
            pl.BlockSpec(memory_space=pltpu.SMEM),
            vmem,
            pl.BlockSpec((1, NLAT, MW), lambda s: (s, 0, 0)),
            vmem,
            vmem,
            vmem,
            vmem,
        ],
        out_specs=pl.BlockSpec(memory_space=pl.ANY),
        scratch_shapes=[
            pltpu.VMEM((10, 256, 256), BF),
            pltpu.VMEM((5120, BLK), F32),
            pltpu.VMEM((2, 256, MW // BLK, 2, BLK), BF),
            pltpu.SemaphoreType.DMA((2, MW // BLK)),
        ],
        compiler_params=pltpu.CompilerParams(vmem_limit_bytes=32 * MIB),
        name="receive",
    )(waves, moved, legendre, ahead, behind, scale, order)


def shards(
    table,
    order,
    grid,
    halo_values,
    halo_owner,
    halo_block,
    halo_count,
    wave_list,
    legendre,
    modes,
    back,
    eigen,
):
    bands = lax.axis_size("wave")
    sent = pack(halo_owner, halo_block, halo_count, halo_values.reshape(SLOTS, 32, BLK))
    came = []
    for message, step in zip(sent, OFFSETS):
        route = [(i, i + step) for i in range(bands) if 0 <= i + step < bands]
        came.append(lax.ppermute(message, "wave", route))
    fourier = dft(grid.reshape(32, 8, NLON), came, wave_list.reshape(10, BLK), table)
    moved = lax.all_to_all(
        fourier.reshape(256, 5, 4, BLK), ("lev", "wave"), split_axis=0, concat_axis=0, tiled=True
    ).reshape(5120, BLK)
    ahead, behind, scale = prepare(modes, back, eigen.reshape(1, LEV))
    result = receive(wave_list, moved, legendre, ahead, behind, scale, order)
    return result.reshape(5, LEV, F, 2, MW)


def solution(mesh):
    placed = (
        P("lev", None, "wave", None),
        P("wave", None, "lev", None, None),
        P("wave", None),
        P("wave", None),
        P("wave"),
        P(),
        P(("lev", "wave"), None, None),
        P(),
        P(),
        P(),
    )
    mapped = jax.shard_map(
        shards,
        mesh=mesh,
        in_specs=(P(), P()) + placed,
        out_specs=P(("lev", "wave"), None, None, None, None),
        check_vma=False,
    )
    table = half_table()
    order = row_order()

    def whole(*args):
        return mapped(jnp.asarray(table), jnp.asarray(order), *args)

    return whole
```

time: 295 us -> 109 us (0.37)
  other arithmetic: 66.5 us -> 0 us
  matrix products: 55.8 us -> 0 us
  local copies, waits for them, and re-layouts: 64.2 us -> 12.5 us
  blocking collectives: 27.3 us -> 0 us
  Pallas kernels: 0 us -> 25.9 us
  starting transfers between devices: 41.5 us -> 32.9 us
    another operation x2 -> x0, other arithmetic: 63.7 us -> none
    dot_general x7 -> x0, matrix products: 55.8 us -> none  [the longest x1 19.1 us: vertical(): jnp.einsum('skfcn,ki->sifcn', coefficient, modes, precision=lax.Precision...]
    all_to_all x1 -> x0, blocking collectives: 27.3 us -> none  [shards(): lax.all_to_all(fourier, 'lev', split_axis=0, concat_axis=2, tiled=True)]
    pallas_call x0 -> x4, Pallas kernels: none -> 25.9 us  [the longest x1 13.6 us: receive(): pl.pallas_call(receive_kernel, grid=(5,), out_shape=jax.ShapeDtypeStruct(...]
    reshape x3 -> x0, local copies, waits for them, and re-layouts: 25.7 us -> none  [the longest x1 15.7 us: shards(): coefficient = coefficient.reshape(slot_dev, levels, F, 2, MW)]
    convert_element_type x2 -> x0, local copies, waits for them, and re-layouts: 15.5 us -> none  [the longest x1 14.3 us: shards(): return vertical(coefficient, modes, back, eigen, MW).astype(jnp.bfloat16)]
    ppermute x8 -> x4, starting transfers between devices: 26.3 us -> 13.3 us  [shards(): came.append(lax.ppermute(message, 'wave', route))]
    all_to_all x2 -> x0, local copies, waits for them, and re-layouts: 10.8 us -> none  [shards(): lax.all_to_all(fourier, 'lev', split_axis=0, concat_axis=2, tiled=True)]
  transfers between devices with their start and end apart: 9 -> 5, of which waited for: 4 -> 2; matrix products, arithmetic and copies ran while one was open for 24% -> 0% of each run, Pallas kernels for 0% -> 0%
where the time goes in v1:
time: 109 us; the launch traced here: 108 us
  waiting for transfers between devices  36.3 us (33%)
  starting transfers between devices  32.9 us (30%)
  Pallas kernels  25.9 us (24%)
  local copies, waits for them, and re-layouts  12.5 us (11%)
    all_to_all x1, waiting for transfers between devices, shards(): lax.all_to_all(fourier.reshape(256, 5, 4, BLK), ('lev', 'wave'), split_ax...  34.9 us
    all_to_all x1, starting transfers between devices, shards(): lax.all_to_all(fourier.reshape(256, 5, 4, BLK), ('lev', 'wave'), split_ax...  19.6 us
    pallas_call x1, Pallas kernels, receive(): pl.pallas_call(receive_kernel, grid=(5,), out_shape=jax.ShapeDtypeStruct(...  13.6 us
    ppermute x4, starting transfers between devices, shards(): came.append(lax.ppermute(message, 'wave', route))  13.3 us
    unnamed x32, local copies, waits for them, and re-layouts  12.5 us
    pallas_call x1, Pallas kernels, dft(): pl.pallas_call(dft_kernel, out_shape=jax.ShapeDtypeStruct((MW * 4, BLK),...  10.2 us
  transfers between devices with their start and end apart: 5, of which 2 were waited for; matrix products, arithmetic and copies ran while one was open for 0% of the time, Pallas kernels for 0%

profile of v1, /device:TPU:1, one launch (start us, length us, event | category | flops | bytes accessed | tf_op | source)
XLA Modules:
  0.0 108.4 jit_solution(13298397687283736080)
XLA Ops:
  0.7 0.0 copy-start.4
  0.7 1.0 copy-done.4
  1.7 0.0 copy-start.13
  1.7 0.7 copy-done.13
  2.4 0.0 copy-start.14
  2.4 0.7 copy-done.14
  3.0 1.6 %pack.1 = (bf16[272,128]{1,0:T(8,128)(2,1)S(1)}, bf16[272,128]{1,0:T(8,128)(2,1)S(1)}, bf16[272,128]{1,0:T(8,128)(2,1)S(1)}, bf16[272,128]{1,0:T(8,128)(2,1)S(1)}) custom-call(s32[1,32]{1,0:T(1,128)S(1)} %copy-done.13, s32[1,32]{1,0:T(1,128)S(1)} %copy-done.14, s32[1]{0:T(128)S(6)} %copy.13.count, f32[32,32,128]{2,1,0:T(8,128)S(1)} %bitcast.9), custom_call_target="tpu_custom_call" | custom-call | tf_op jit(solution)/shard_map/pack/pallas_call | solution.py:84
  4.6 1.3 %collective-permute-start = (bf16[272,128]{1,0:T(8,128)(2,1)S(1)}, bf16[272,128]{1,0:T(8,128)(2,1)S(1)}, u32[]{:S(2)}, u32[]{:S(2)}) collective-permute-start(bf16[272,128]{1,0:T(8,128)(2,1)S(1)} %get-tuple-element.12), channel_id=1, source_target_pairs={{2,0},{3,1},{4,2},{5,3},{6,4},{7,5},{8,6},{9,7},{10,8},{11,9},{12,... | collective-permute-start | bytes 208904 | tf_op jit(solution)/shard_map/ppermute | solution.py:309
  5.9 1.3 %collective-permute-start.1 = (bf16[272,128]{1,0:T(8,128)(2,1)S(1)}, bf16[272,128]{1,0:T(8,128)(2,1)S(1)}, u32[]{:S(2)}, u32[]{:S(2)}) collective-permute-start(bf16[272,128]{1,0:T(8,128)(2,1)S(1)} %get-tuple-element.13), channel_id=1, source_target_pairs={{1,0},{2,1},{3,2},{4,3},{5,4},{6,5},{7,6},{8,7},{9,8},{10,9},{11,1... | collective-permute-start | bytes 208904 | tf_op jit(solution)/shard_map/ppermute | solution.py:309
  7.2 4.7 %collective-permute-start.2 = (bf16[272,128]{1,0:T(8,128)(2,1)S(1)}, bf16[272,128]{1,0:T(8,128)(2,1)S(1)}, u32[]{:S(2)}, u32[]{:S(2)}) collective-permute-start(bf16[272,128]{1,0:T(8,128)(2,1)S(1)} %get-tuple-element.14), channel_id=1, source_target_pairs={{0,1},{1,2},{2,3},{3,4},{4,5},{5,6},{6,7},{7,8},{8,9},{9,10},{10,1... | collective-permute-start | bytes 208904 | tf_op jit(solution)/shard_map/ppermute | solution.py:309
  11.9 6.1 %collective-permute-start.3 = (bf16[272,128]{1,0:T(8,128)(2,1)S(1)}, bf16[272,128]{1,0:T(8,128)(2,1)S(1)}, u32[]{:S(2)}, u32[]{:S(2)}) collective-permute-start(bf16[272,128]{1,0:T(8,128)(2,1)S(1)} %get-tuple-element.15), channel_id=1, source_target_pairs={{0,2},{1,3},{2,4},{3,5},{4,6},{5,7},{6,8},{7,9},{8,10},{9,11},{10,... | collective-permute-start | bytes 208904 | tf_op jit(solution)/shard_map/ppermute | solution.py:309
  18.0 0.0 collective-permute-done.m0
  18.0 0.0 collective-permute-done.1.m1
  18.0 0.0 collective-permute-done.2.m2
  18.0 1.3 %collective-permute-done.3.m3 = bf16[272,128]{1,0:T(8,128)(2,1)S(1)} collective-permute-done((bf16[272,128]{1,0:T(8,128)(2,1)S(1)}, bf16[272,128]{1,0:T(8,128)(2,1)S(1)}, u32[]{:S(2)}, u32[]{:S(2)}) %collective-permute-start.3) | collective-permute-done | bytes 69664 | tf_op jit(solution)/shard_map/ppermute | solution.py:309
  19.3 0.0 copy-start
  19.3 3.0 %copy-done = bf16[2,2,640,1408]{3,2,1,0:T(8,128)(2,1)S(1)} copy-done((bf16[2,2,640,1408]{3,2,1,0:T(8,128)(2,1)S(1)}, bf16[2,2,640,1408]{3,2,1,0:T(8,128)(2,1)}, u32[]{:S(2)}) %copy-start) | copy-done | bytes 7208984
  22.4 0.0 copy-start.2
  22.4 1.4 %copy-done.2 = bf16[8,4,8,2816]{3,2,1,0:T(8,128)(2,1)S(1)} copy-done((bf16[8,4,8,2816]{3,2,1,0:T(8,128)(2,1)S(1)}, bf16[8,4,8,2816]{3,2,1,0:T(8,128)(2,1)}, u32[]{:S(2)}) %copy-start.2) | copy-done | bytes 1441816
  23.8 0.0 copy-start.11
  23.8 0.7 copy-done.11
  24.4 10.2 %dft.1 = bf16[5120,128]{1,0:T(8,128)(2,1)} custom-call(bf16[32,8,2816]{2,1,0:T(8,128)(2,1)S(1)} %bitcast.8, bf16[272,128]{1,0:T(8,128)(2,1)S(1)} %collective-permute-done.m0, bf16[272,128]{1,0:T(8,128)(2,1)S(1)} %collective-permute-done.1.m1, bf16[272,128]{1,0:T(8,128)(2,1)S(1)} %collective-permute-done.2.m2, ...), custom_call_target="tpu_custom_call" | custom-call | tf_op jit(solution)/shard_map/dft/pallas_call | solution.py:148
  34.7 0.0 copy-start.9
  34.7 0.0 copy-start.10
  34.7 0.0 copy-start.15
  34.7 0.0 copy-start.3
  34.7 0.0 copy-start.12
  34.7 19.6 %all-to-all-start = ((bf16[256,5,4,128]{3,2,1,0:T(4,128)(2,1)}), bf16[256,5,4,128]{3,2,1,0:T(4,128)(2,1)S(1)}, u32[]{:S(2)}, u32[]{:S(2)}) async-start(bf16[256,5,4,128]{3,2,1,0:T(4,128)(2,1)} %bitcast.3), calls=%async_computation | async-start | bytes 2621440 | tf_op jit(solution)/shard_map/all_to_all | solution.py:311
  54.3 0.0 copy-done.9
  54.3 0.0 copy-done.10
  54.3 0.0 copy-done.15
  54.4 0.4 prepare.1
  54.8 0.0 copy-start.5
  54.8 0.6 copy-done.5
  55.5 0.0 copy-start.7
  55.5 0.6 copy-done.7
  56.1 34.9 %all-to-all-done = bf16[256,5,4,128]{3,2,1,0:T(4,128)(2,1)S(1)} async-done(((bf16[256,5,4,128]{3,2,1,0:T(4,128)(2,1)}), bf16[256,5,4,128]{3,2,1,0:T(4,128)(2,1)S(1)}, u32[]{:S(2)}, u32[]{:S(2)}) %all-to-all-start) | async-done | bytes 1310752 | tf_op jit(solution)/shard_map/all_to_all | solution.py:311
  91.1 0.0 copy-done.3
  91.1 0.0 copy-done.12
  91.1 0.0 copy-start.1
  91.1 1.9 %copy-done.1 = bf16[5,256,1280]{2,1,0:T(8,128)(2,1)S(1)} copy-done((bf16[5,256,1280]{2,1,0:T(8,128)(2,1)S(1)}, bf16[5,256,1280]{2,1,0:T(8,128)(2,1)}, u32[]{:S(2)}) %copy-start.1) | copy-done | bytes 3276824
  93.0 0.0 copy-start.6
  93.0 0.9 copy-done.6
  93.9 0.0 copy-start.8
  93.9 0.9 copy-done.8
  94.8 13.6 %receive.1 = bf16[1280,2,1280]{2,1,0:T(2,128)(2,1)} custom-call(s32[1280]{0:T(1024)S(1)} %copy-done.12, bf16[5120,128]{1,0:T(8,128)(2,1)S(1)} %bitcast.7, bf16[5,256,1280]{2,1,0:T(8,128)(2,1)S(1)} %copy-done.1, bf16[256,256]{1,0:T(8,128)(2,1)S(1)} %copy-done.6, bf16[256,256]{1,0:T(8,128)(2,1)S(1)} %copy-done.8, f32[256,1280]{1,0:T(8,128)S(1)} %get-tuple-element.18.scale, ...), custom_call_target="tpu_custom_call" | custom-call | tf_op jit(solution)/shard_map/receive/pallas_call | solution.py:265
Async XLA Ops:
  0.7 1.0 copy-start.4
  1.7 0.7 copy-start.13
  2.4 0.7 copy-start.14
  4.6 13.4 %collective-permute-start = (bf16[272,128]{1,0:T(8,128)(2,1)S(1)}, bf16[272,128]{1,0:T(8,128)(2,1)S(1)}, u32[]{:S(2)}, u32[]{:S(2)}) collective-permute-start(bf16[272,128]{1,0:T(8,128)(2,1)S(1)} %get-tuple-element.12), channel_id=1, source_target_pairs={{2,0},{3,1},{4,2},{5,3},{6,4},{7,5},{8,6},{9,7},{10,8},{11,9},{12,... | collective-permute-start | bytes 208904 | tf_op jit(solution)/shard_map/ppermute | solution.py:309
  5.9 12.1 %collective-permute-start.1 = (bf16[272,128]{1,0:T(8,128)(2,1)S(1)}, bf16[272,128]{1,0:T(8,128)(2,1)S(1)}, u32[]{:S(2)}, u32[]{:S(2)}) collective-permute-start(bf16[272,128]{1,0:T(8,128)(2,1)S(1)} %get-tuple-element.13), channel_id=1, source_target_pairs={{1,0},{2,1},{3,2},{4,3},{5,4},{6,5},{7,6},{8,7},{9,8},{10,9},{11,1... | collective-permute-start | bytes 208904 | tf_op jit(solution)/shard_map/ppermute | solution.py:309
  7.2 10.8 %collective-permute-start.2 = (bf16[272,128]{1,0:T(8,128)(2,1)S(1)}, bf16[272,128]{1,0:T(8,128)(2,1)S(1)}, u32[]{:S(2)}, u32[]{:S(2)}) collective-permute-start(bf16[272,128]{1,0:T(8,128)(2,1)S(1)} %get-tuple-element.14), channel_id=1, source_target_pairs={{0,1},{1,2},{2,3},{3,4},{4,5},{5,6},{6,7},{7,8},{8,9},{9,10},{10,1... | collective-permute-start | bytes 208904 | tf_op jit(solution)/shard_map/ppermute | solution.py:309
  11.9 7.5 %collective-permute-start.3 = (bf16[272,128]{1,0:T(8,128)(2,1)S(1)}, bf16[272,128]{1,0:T(8,128)(2,1)S(1)}, u32[]{:S(2)}, u32[]{:S(2)}) collective-permute-start(bf16[272,128]{1,0:T(8,128)(2,1)S(1)} %get-tuple-element.15), channel_id=1, source_target_pairs={{0,2},{1,3},{2,4},{3,5},{4,6},{5,7},{6,8},{7,9},{8,10},{9,11},{10,... | collective-permute-start | bytes 208904 | tf_op jit(solution)/shard_map/ppermute | solution.py:309
  19.3 3.0 %copy-start = (bf16[2,2,640,1408]{3,2,1,0:T(8,128)(2,1)S(1)}, bf16[2,2,640,1408]{3,2,1,0:T(8,128)(2,1)}, u32[]{:S(2)}) copy-start(bf16[2,2,640,1408]{3,2,1,0:T(8,128)(2,1)} %constant.4.clone.table) | copy-start | bytes 21626884
  22.4 1.4 %copy-start.2 = (bf16[8,4,8,2816]{3,2,1,0:T(8,128)(2,1)S(1)}, bf16[8,4,8,2816]{3,2,1,0:T(8,128)(2,1)}, u32[]{:S(2)}) copy-start(bf16[8,4,8,2816]{3,2,1,0:T(8,128)(2,1)} %param.12) | copy-start | bytes 4325380
  23.8 0.7 copy-start.11
  34.7 19.7 %copy-start.9 = (f32[64,64]{1,0:T(8,128)S(1)}, f32[64,64]{1,0:T(8,128)}, u32[]{:S(2)}) copy-start(f32[64,64]{1,0:T(8,128)} %modes.1) | copy-start | bytes 49156
  34.7 19.7 %copy-start.10 = (f32[64,64]{1,0:T(8,128)S(1)}, f32[64,64]{1,0:T(8,128)}, u32[]{:S(2)}) copy-start(f32[64,64]{1,0:T(8,128)} %back.1) | copy-start | bytes 49156
  34.7 19.7 %copy-start.15 = (f32[64]{0:T(128)S(1)}, f32[64]{0:T(128)}, u32[]{:S(2)}) copy-start(f32[64]{0:T(128)} %param.21) | copy-start | bytes 772
  34.7 56.4 %copy-start.3 = (bf16[640,640]{1,0:T(8,128)(2,1)S(1)}, bf16[640,640]{1,0:T(8,128)(2,1)}, u32[]{:S(2)}) copy-start(bf16[640,640]{1,0:T(8,128)(2,1)} %constant.5.clone.order) | copy-start | bytes 2457604
  34.7 56.3 %copy-start.12 = (s32[1280]{0:T(1024)S(1)}, s32[1280]{0:T(1024)}, u32[]{:S(2)}) copy-start(s32[1280]{0:T(1024)} %waves.1) | copy-start | bytes 15364
  34.7 56.3 %all-to-all-start = ((bf16[256,5,4,128]{3,2,1,0:T(4,128)(2,1)}), bf16[256,5,4,128]{3,2,1,0:T(4,128)(2,1)S(1)}, u32[]{:S(2)}, u32[]{:S(2)}) async-start(bf16[256,5,4,128]{3,2,1,0:T(4,128)(2,1)} %bitcast.3), calls=%async_computation | async-start | bytes 2621440 | tf_op jit(solution)/shard_map/all_to_all | solution.py:311
  54.8 0.7 copy-start.5
  55.5 0.7 copy-start.7
  91.1 1.9 %copy-start.1 = (bf16[5,256,1280]{2,1,0:T(8,128)(2,1)S(1)}, bf16[5,256,1280]{2,1,0:T(8,128)(2,1)}, u32[]{:S(2)}) copy-start(bf16[5,256,1280]{2,1,0:T(8,128)(2,1)} %legendre.1) | copy-start | bytes 9830404
  93.0 0.9 copy-start.6
  93.9 0.9 copy-start.8

commit v2 on v1

v2 whole, which is shorter than its diff:
```python
import math

import jax
import jax.numpy as jnp
import ml_dtypes
import numpy as np
from jax import lax
from jax.experimental import pallas as pl
from jax.experimental.pallas import tpu as pltpu
from jax.sharding import PartitionSpec as P

MW = 1280
NLON = 2816
F = 4
LEV = 64
BLK = 128
CAP = 8
REACH = 2
SLOTS = 32
NLAT = 256
HALF = NLON // 2
CHUNKS = NLON // BLK
OFFSETS = (-2, -1, 1, 2)
MSG = CAP * 32 + 16
BF = jnp.bfloat16
F32 = jnp.float32

MIB = 1 << 20


def half_table():
    order = np.arange(MW, dtype=np.int64).reshape(MW // 2, 2).T
    phase = order[:, :, None] * np.arange(HALF, dtype=np.int64)[None, None, :] % NLON
    angle = phase.astype(np.float32) * np.float32(2.0 * math.pi / NLON)
    scale = np.float32(1.0 / math.sqrt(NLON))
    both = np.stack([np.cos(angle) * scale, -np.sin(angle) * scale], 1)
    return both.reshape(2, MW, HALF).astype(ml_dtypes.bfloat16)


def dot(a, b):
    return lax.dot_general(a, b, (((1,), (0,)), ((), ())), preferred_element_type=F32)


def dot_nt(a, b):
    return lax.dot_general(a, b, (((1,), (1,)), ((), ())), preferred_element_type=F32)


def pack_kernel(owner, block, count, values, *refs):
    outs = refs[:4]
    owner_s, block_s, count_s, held, lists, used, sems = refs[4:]
    copies = [
        pltpu.make_async_copy(source, target, sems.at[i])
        for i, (source, target) in enumerate(
            ((owner, owner_s), (block, block_s), (count, count_s), (values, held))
        )
    ]
    for copy in copies:
        copy.start()
    band = lax.axis_index("wave")
    for number in range(5):
        used[number] = 0
    for copy in copies[:3]:
        copy.wait()
    for slot in range(SLOTS):
        step = owner_s[0, slot] - band
        number = jnp.where(step < 0, step + REACH, step + REACH - 1)
        number = jnp.where(slot < count_s[0], jnp.clip(number, 0, 4), 4)
        at = used[number]
        lists[number, at] = slot
        used[number] = at + 1
    row = lax.broadcasted_iota(jnp.int32, (16, BLK), 0)
    copies[3].wait()
    for number, out in enumerate(outs):
        marks = jnp.zeros((16, BLK), F32)
        for at in range(CAP):
            valid = at < used[number]
            slot = jnp.where(valid, lists[number, at], 0)
            out[at * 32 : (at + 1) * 32, :] = jnp.where(valid, held[slot], 0.0).astype(BF)
            which = jnp.where(valid, block_s[0, slot], 0).astype(F32)
            marks = jnp.where(row == at, which, marks)
        out[CAP * 32 :, :] = marks.astype(BF)


def params(flops=0, read=0, room=60):
    return dict(
        compiler_params=pltpu.CompilerParams(vmem_limit_bytes=room * MIB),
        cost_estimate=pl.CostEstimate(flops=flops, bytes_accessed=read, transcendentals=0),
    )


def pack(owner, block, count, values):
    vmem = pl.BlockSpec(memory_space=pltpu.VMEM)
    return pl.pallas_call(
        pack_kernel,
        out_shape=[jax.ShapeDtypeStruct((MSG, BLK), BF)] * 4,
        in_specs=[pl.BlockSpec(memory_space=pl.ANY)] * 4,
        out_specs=[vmem] * 4,
        scratch_shapes=[
            pltpu.SMEM((1, SLOTS), jnp.int32),
            pltpu.SMEM((1, SLOTS), jnp.int32),
            pltpu.SMEM((1,), jnp.int32),
            pltpu.VMEM((SLOTS, 32, BLK), F32),
            pltpu.SMEM((5, SLOTS), jnp.int32),
            pltpu.SMEM((5,), jnp.int32),
            pltpu.SemaphoreType.DMA((4,)),
        ],
        name="pack",
        **params(read=1 << 20),
    )(owner, block, count, values)


def ready_kernel(grid, out, held, made, sems):
    parts = [
        pltpu.make_async_copy(grid.at[pl.ds(16 * i, 16)], held.at[pl.ds(16 * i, 16)], sems.at[i])
        for i in range(2)
    ]
    for part in parts:
        part.start()
    for i, part in enumerate(parts):
        part.wait()
        for c in range(CHUNKS):
            block = held[16 * i : 16 * i + 16, :, c * BLK : (c + 1) * BLK].astype(F32)
            block = jnp.swapaxes(block, 0, 1).astype(BF)
            for j in range(8):
                made[c, j * 32 + 16 * i : j * 32 + 16 * i + 16, :] = block[j]
    back = pltpu.make_async_copy(made, out, sems.at[2])
    back.start()
    back.wait()


def ready(grid):
    hbm = pl.BlockSpec(memory_space=pl.ANY)
    return pl.pallas_call(
        ready_kernel,
        out_shape=jax.ShapeDtypeStruct((CHUNKS, 256, BLK), BF),
        in_specs=[hbm],
        out_specs=hbm,
        scratch_shapes=[
            pltpu.VMEM((32, 8, NLON), BF),
            pltpu.VMEM((CHUNKS, 256, BLK), BF),
            pltpu.SemaphoreType.DMA((3,)),
        ],
        name="ready",
        **params(read=3 << 20),
    )(grid)


def dft_kernel(
    m0, m1, m2, m3, waves, rows, table, out, raw, acc, pick, surf, held, four, strided, got, marks, marks_s, sems
):
    messages = (m0, m1, m2, m3)
    from_far = [
        pltpu.make_async_copy(message, got.at[i], sems.at[i]) for i, message in enumerate(messages)
    ]
    from_grid = pltpu.make_async_copy(rows, raw, sems.at[4])
    from_table = [
        pltpu.make_async_copy(table.at[p], held.at[p], sems.at[5 + p]) for p in range(2)
    ]
    for copy in from_far + [from_grid, from_table[0]]:
        copy.start()
    for number, copy in enumerate(from_far):
        copy.wait()
        marks[pl.ds(number * CAP, CAP), :] = (
            got[number, pl.ds(CAP * 32, 16), :].astype(F32)[:CAP].astype(jnp.int32)
        )
    to_scalar = pltpu.make_async_copy(marks, marks_s, sems.at[7])
    to_scalar.start()
    from_grid.wait()
    from_table[1].start()
    acc[...] = raw[...].astype(F32)
    to_scalar.wait()
    for number in range(4):
        for r in range(CAP):
            b = marks_s[number * CAP + r, 0]
            j = b // CHUNKS
            c = b - j * CHUNKS
            at = pl.ds(pl.multiple_of(j * 32, 32), 32)
            acc[c, at, :] = acc[c, at, :] + got[number, pl.ds(r * 32, 32), :].astype(F32)
    for c in range(CHUNKS // 2):
        near, far = acc[c], acc[c + CHUNKS // 2]
        surf[0, :, c * BLK : (c + 1) * BLK] = (near + far).astype(BF)
        surf[1, :, c * BLK : (c + 1) * BLK] = (near - far).astype(BF)
    half = MW // 2
    column = lax.broadcasted_iota(jnp.int32, (BLK, BLK), 1)
    for p in range(2):
        from_table[p].wait()
        both = dot_nt(held[p], surf[p]).astype(BF)
        for b in range(p * 5, p * 5 + 5):
            m = waves[b : b + 1, :]
            key = (m % 2) * half + m // 2
            key = jnp.broadcast_to(key.astype(F32), (BLK, BLK)).T.astype(jnp.int32)
            for t in range(MW // BLK):
                pick[b * BLK : (b + 1) * BLK, t * BLK : (t + 1) * BLK] = jnp.where(
                    key == column + t * BLK, 1.0, 0.0
                ).astype(BF)
        for part in range(2):
            four[p * half : (p + 1) * half, part * 256 : (part + 1) * 256] = both[
                part * half : (part + 1) * half
            ]
    for b in range(2):
        found = dot(pick[b * half : (b + 1) * half], four[...])
        for q in range(4):
            strided[b, pl.ds(q, half, stride=4), :] = found[:, q * BLK : (q + 1) * BLK]
        out[b * 4 * half : (b + 1) * 4 * half, :] = strided[b].astype(BF)


def dft(messages, waves, rows, table):
    hbm = pl.BlockSpec(memory_space=pl.ANY)
    vmem = pl.BlockSpec(memory_space=pltpu.VMEM)
    return pl.pallas_call(
        dft_kernel,
        out_shape=jax.ShapeDtypeStruct((MW * 4, BLK), BF),
        in_specs=[hbm] * 4 + [vmem, hbm, hbm],
        out_specs=vmem,
        scratch_shapes=[
            pltpu.VMEM((CHUNKS, 256, BLK), BF),
            pltpu.VMEM((CHUNKS, 256, BLK), F32),
            pltpu.VMEM((MW, MW), BF),
            pltpu.VMEM((2, 256, HALF), BF),
            pltpu.VMEM((2, MW, HALF), BF),
            pltpu.VMEM((MW, 512), BF),
            pltpu.VMEM((2, MW * 2, BLK), F32),
            pltpu.VMEM((4, MSG, BLK), BF),
            pltpu.VMEM((SLOTS, BLK), jnp.int32),
            pltpu.SMEM((SLOTS, BLK), jnp.int32),
            pltpu.SemaphoreType.DMA((8,)),
        ],
        name="dft",
        **params(flops=4 << 30, read=16 << 20, room=60),
    )(*messages, waves, rows, table)


def prepare_kernel(modes, back, eigen, legendre, ahead, behind, scale, turned):
    row = lax.broadcasted_iota(jnp.int32, (256, 256), 0)
    place = lax.rem(row, 32) * 8 + lax.rem(row // 32, 2) * 4 + row // 64
    move = jnp.where(place == lax.broadcasted_iota(jnp.int32, (256, 256), 1), 1.0, 0.0)
    turned[0] = dot(move.astype(BF), legendre[0]).astype(BF)

    @pl.when(pl.program_id(0) == 0)
    def _():
        spread = jnp.where(
            lax.broadcasted_iota(jnp.int32, (256, LEV), 0) // F
            == lax.broadcasted_iota(jnp.int32, (256, LEV), 1),
            1.0,
            0.0,
        )
        picks = spread.astype(BF)
        row = lax.broadcasted_iota(jnp.int32, (256, 256), 0)
        column = lax.broadcasted_iota(jnp.int32, (256, 256), 1)
        same = lax.rem(row, F) == lax.rem(column, F)
        rows = dot_nt(picks, modes[...].astype(BF)).astype(BF)
        ahead[...] = jnp.where(same, dot_nt(rows, picks), 0.0).astype(BF)
        rows = dot_nt(picks, back[...].astype(BF)).astype(BF)
        single = jnp.where(same, dot_nt(rows, picks), 0.0).astype(BF)
        row = lax.broadcasted_iota(jnp.int32, (512, 256), 0)
        column = lax.broadcasted_iota(jnp.int32, (512, 256), 1)
        for part in range(2):
            chosen = jnp.where(row == column * 2 + part, 1.0, 0.0).astype(BF)
            behind[:, part * 256 : (part + 1) * 256] = dot(chosen, single).astype(BF)
        value = jnp.sum(spread * eigen[...], axis=1, keepdims=True)
        order = lax.broadcasted_iota(jnp.int32, (1, MW), 1).astype(F32)
        ratio = order * (order + 1.0) / (MW * (MW - 1.0))
        scale[...] = 1.0 / (1.0 + value * ratio)


def prepare(modes, back, eigen, legendre):
    def whole(*shape):
        return pl.BlockSpec(shape, lambda s: (0,) * len(shape))

    return pl.pallas_call(
        prepare_kernel,
        grid=(5,),
        out_shape=[
            jax.ShapeDtypeStruct((256, 256), BF),
            jax.ShapeDtypeStruct((512, 512), BF),
            jax.ShapeDtypeStruct((256, MW), F32),
            jax.ShapeDtypeStruct((5, NLAT, MW), BF),
        ],
        in_specs=[
            whole(LEV, LEV),
            whole(LEV, LEV),
            whole(1, LEV),
            pl.BlockSpec((1, NLAT, MW), lambda s: (s, 0, 0)),
        ],
        out_specs=[
            whole(256, 256),
            whole(512, 512),
            whole(256, MW),
            pl.BlockSpec((1, NLAT, MW), lambda s: (s, 0, 0)),
        ],
        name="prepare",
        **params(flops=2 << 30, read=8 << 20),
    )(modes, back, eigen, legendre)


def receive_kernel(
    waves, moved, legendre, ahead, behind, scale, out, *scratch
):
    moved_v, legendre_v, ahead_v, behind_v, scale_v, spread, latitude, projected, made, sems, sems_out = scratch
    first_copies = [
        pltpu.make_async_copy(moved.at[pl.ds(640 * lev, 640)], moved_v.at[pl.ds(640 * lev, 640)], sems.at[lev])
        for lev in range(8)
    ]
    later = [
        pltpu.make_async_copy(source, target, sems.at[8 + i])
        for i, (source, target) in enumerate(
            ((ahead, ahead_v), (scale, scale_v), (behind, behind_v))
        )
    ]
    tables = [
        pltpu.make_async_copy(legendre.at[s], legendre_v.at[s], sems.at[11 + s]) for s in range(5)
    ]
    for copy in first_copies + later + tables:
        copy.start()
    for copy in first_copies:
        copy.wait()
    for j in range(4):
        for lanes in range(2):
            mixed = jnp.concatenate(
                [
                    moved_v[lev * 640 : (lev + 1) * 640, j * 32 : (j + 1) * 32]
                    for lev in range(lanes * 4, lanes * 4 + 4)
                ],
                1,
            )
            spread[j, lanes] = mixed.astype(F32)

    def gather(s):
        for part in range(2):
            for j in range(4):
                for jq in range(2):
                    for lanes in range(2):
                        at = part * 256 + j * 64 + jq * 32
                        latitude[s, at : at + 32, lanes * BLK : (lanes + 1) * BLK] = spread[
                            j, lanes, pl.ds((2 * s + part) * 2 + jq, 32, stride=20), :
                        ].astype(BF)

    def project(s):
        projected[s] = dot_nt(ahead_v[...], latitude[s]).astype(BF)

    gather(0)
    later[0].wait()
    project(0)
    later[1].wait()
    later[2].wait()
    first = (lax.axis_index("lev") * 32 + lax.axis_index("wave")) * 5
    order = lax.broadcasted_iota(jnp.int32, (1, MW), 1)
    sends = []
    for s in range(5):
        tables[s].wait()
        if s < 4:
            gather(s + 1)
        factor = jnp.where(order >= waves[first + s], scale_v[...], 0.0)
        scaled = [
            (dot(projected[s, :, part * 256 : (part + 1) * 256], legendre_v[s]) * factor).astype(BF)
            for part in range(2)
        ]
        made.at[s].reshape(512, MW)[...] = dot(behind_v[...], jnp.concatenate(scaled, 0)).astype(BF)
        send = pltpu.make_async_copy(made.at[s], out.at[pl.ds(s * 256, 256)], sems_out.at[s])
        send.start()
        sends.append(send)
        if s < 4:
            project(s + 1)
    for send in sends:
        send.wait()


def receive(waves, moved, legendre, ahead, behind, scale):
    hbm = pl.BlockSpec(memory_space=pl.ANY)
    return pl.pallas_call(
        receive_kernel,
        out_shape=jax.ShapeDtypeStruct((5 * 256, 2, MW), BF),
        in_specs=[pl.BlockSpec(memory_space=pltpu.SMEM)] + [hbm] * 5,
        out_specs=hbm,
        scratch_shapes=[
            pltpu.VMEM((5120, BLK), BF),
            pltpu.VMEM((5, NLAT, MW), BF),
            pltpu.VMEM((256, 256), BF),
            pltpu.VMEM((512, 512), BF),
            pltpu.VMEM((256, MW), F32),
            pltpu.VMEM((4, 2, 640, BLK), F32),
            pltpu.VMEM((5, 512, 256), BF),
            pltpu.VMEM((5, 256, 512), BF),
            pltpu.VMEM((5, 256, 2, MW), BF),
            pltpu.SemaphoreType.DMA((16,)),
            pltpu.SemaphoreType.DMA((5,)),
        ],
        name="receive",
        **params(flops=6 << 30, read=14 << 20, room=60),
    )(waves, moved, legendre, ahead, behind, scale)


def shards(
    table, grid, halo_values, halo_owner, halo_block, halo_count, wave_list, legendre, modes, back, eigen
):
    bands = lax.axis_size("wave")
    sent = pack(halo_owner, halo_block, halo_count, halo_values.reshape(SLOTS, 32, BLK))
    came = []
    for message, step in zip(sent, OFFSETS):
        route = [(i, (i + step) % bands) for i in range(bands)]
        came.append(lax.ppermute(message, "wave", route))
    grid, _ = lax.optimization_barrier((grid, sent))
    rows = ready(grid.reshape(32, 8, NLON))
    fourier = dft(came, wave_list.reshape(10, BLK), rows, table)
    moved = lax.all_to_all(
        fourier.reshape(256, 5, 4, BLK), ("lev", "wave"), split_axis=0, concat_axis=0, tiled=True
    ).reshape(5120, BLK)
    legendre, _ = lax.optimization_barrier((legendre, fourier))
    ahead, behind, scale, turned = prepare(modes, back, eigen.reshape(1, LEV), legendre)
    result = receive(wave_list, moved, turned, ahead, behind, scale)
    return result.reshape(5, LEV, F, 2, MW)


def solution(mesh):
    placed = (
        P("lev", None, "wave", None),
        P("wave", None, "lev", None, None),
        P("wave", None),
        P("wave", None),
        P("wave"),
        P(),
        P(("lev", "wave"), None, None),
        P(),
        P(),
        P(),
    )
    mapped = jax.shard_map(
        shards,
        mesh=mesh,
        in_specs=(P(),) + placed,
        out_specs=P(("lev", "wave"), None, None, None, None),
        check_vma=False,
    )
    table = half_table()

    def whole(*args):
        return mapped(jnp.asarray(table), *args)

    return whole
```

time: 109 us -> 91 us (0.83)
  starting transfers between devices: 32.9 us -> 20.7 us
  local copies, waits for them, and re-layouts: 12.5 us -> 1.7 us
  Pallas kernels: 25.9 us -> 34.5 us
  waiting for transfers between devices: 36.3 us -> 32.8 us
    unnamed x32 -> x10, local copies, waits for them, and re-layouts: 12.5 us -> 1.7 us
    all_to_all x1, starting transfers between devices: 19.6 us -> 9.37 us  [shards(): lax.all_to_all(fourier.reshape(256, 5, 4, BLK), ('lev', 'wave'), split_ax...]
    pallas_call x2 -> x3, Pallas kernels: 14.1 us -> 21.6 us  [the longest x1 11.4 us: receive(): pl.pallas_call(receive_kernel, out_shape=jax.ShapeDtypeStruct((5 * 256, 2...]
    all_to_all x1, waiting for transfers between devices: 34.9 us -> 29.4 us  [shards(): lax.all_to_all(fourier.reshape(256, 5, 4, BLK), ('lev', 'wave'), split_ax...]
    ppermute x4, waiting for transfers between devices: 1.33 us -> 3.39 us  [shards(): came.append(lax.ppermute(message, 'wave', route))]
    ppermute x4, starting transfers between devices: 13.3 us -> 11.3 us  [shards(): came.append(lax.ppermute(message, 'wave', route))]
  transfers between devices with their start and end apart: 5 -> 5, of which waited for: 2 -> 3; matrix products, arithmetic and copies ran while one was open for 0% -> 0% of each run, Pallas kernels for 0% -> 11%
where the time goes in v2:
time: 91 us; the launch traced here: 90.6 us
  Pallas kernels  34.5 us (38%)
  waiting for transfers between devices  32.8 us (36%)
  starting transfers between devices  20.7 us (23%)
  local copies, waits for them, and re-layouts  1.7 us (2%)
    all_to_all x1, waiting for transfers between devices, shards(): lax.all_to_all(fourier.reshape(256, 5, 4, BLK), ('lev', 'wave'), split_ax...  29.4 us
    pallas_call x1, Pallas kernels, receive(): pl.pallas_call(receive_kernel, out_shape=jax.ShapeDtypeStruct((5 * 256, 2...  11.4 us
    ppermute x4, starting transfers between devices, shards(): came.append(lax.ppermute(message, 'wave', route))  11.3 us
    pallas_call x1, Pallas kernels, dft(): pl.pallas_call(dft_kernel, out_shape=jax.ShapeDtypeStruct((MW * 4, BLK),...  11.1 us
    all_to_all x1, starting transfers between devices, shards(): lax.all_to_all(fourier.reshape(256, 5, 4, BLK), ('lev', 'wave'), split_ax...  9.37 us
    pallas_call x1, Pallas kernels, prepare(): pl.pallas_call(prepare_kernel, grid=(5,), out_shape=[jax.ShapeDtypeStruct...  7.28 us
    ppermute x4, waiting for transfers between devices, shards(): came.append(lax.ppermute(message, 'wave', route))  3.39 us
    pallas_call x1, Pallas kernels, ready(): pl.pallas_call(ready_kernel, out_shape=jax.ShapeDtypeStruct((CHUNKS, 256,...  2.86 us
  transfers between devices with their start and end apart: 5, of which 3 were waited for; matrix products, arithmetic and copies ran while one was open for 0% of the time, Pallas kernels for 11%

profile of v2, /device:TPU:1, one launch (start us, length us, event | category | flops | bytes accessed | tf_op | source)
XLA Modules:
  0.0 90.6 jit_solution(4761264705334093926)
XLA Ops:
  0.7 1.9 %pack.1 = (bf16[272,128]{1,0:T(8,128)(2,1)}, bf16[272,128]{1,0:T(8,128)(2,1)}, bf16[272,128]{1,0:T(8,128)(2,1)}, bf16[272,128]{1,0:T(8,128)(2,1)}) custom-call(s32[1,32]{1,0:T(1,128)} %owner.1, s32[1,32]{1,0:T(1,128)} %block.1, s32[1]{0:T(128)S(6)} %copy.12.count, f32[32,32,128]{2,1,0:T(8,128)} %bitcast.10), custom_call_target="tpu_custom_call" | custom-call | bytes 1048576 | tf_op jit(solution)/shard_map/pack/pallas_call | solution.py:93
  2.5 9.1 %collective-permute-start = (bf16[272,128]{1,0:T(8,128)(2,1)}, bf16[272,128]{1,0:T(8,128)(2,1)S(1)}, u32[]{:S(2)}, u32[]{:S(2)}) collective-permute-start(bf16[272,128]{1,0:T(8,128)(2,1)} %get-tuple-element.15), channel_id=1, source_target_pairs={{0,30},{1,31},{2,0},{3,1},{4,2},{5,3},{6,4},{7,5},{8,6},{9,7},{10,... | collective-permute-start | bytes 208904 | tf_op jit(solution)/shard_map/ppermute | solution.py:401
  11.6 0.8 collective-permute-start.1
  12.4 0.7 collective-permute-start.2
  13.1 0.7 collective-permute-start.3
  13.8 2.9 %ready.1.rows = bf16[22,256,128]{2,1,0:T(8,128)(2,1)} custom-call(bf16[32,8,2816]{2,1,0:T(8,128)(2,1)} %bitcast.7), custom_call_target="tpu_custom_call" | custom-call | bytes 3145728 | tf_op jit(solution)/shard_map/ready/pallas_call | solution.py:133
  16.7 0.0 collective-permute-done.m0
  16.7 0.0 copy-start.1
  16.7 0.0 collective-permute-done.1.m1
  16.7 0.0 copy-start.2
  16.7 2.4 %collective-permute-done.2.m2 = bf16[272,128]{1,0:T(8,128)(2,1)S(1)} collective-permute-done((bf16[272,128]{1,0:T(8,128)(2,1)}, bf16[272,128]{1,0:T(8,128)(2,1)S(1)}, u32[]{:S(2)}, u32[]{:S(2)}) %collective-permute-start.2) | collective-permute-done | bytes 69664 | tf_op jit(solution)/shard_map/ppermute | solution.py:401
  19.1 0.0 copy-start.3
  19.1 1.0 %collective-permute-done.3.m3 = bf16[272,128]{1,0:T(8,128)(2,1)S(1)} collective-permute-done((bf16[272,128]{1,0:T(8,128)(2,1)}, bf16[272,128]{1,0:T(8,128)(2,1)S(1)}, u32[]{:S(2)}, u32[]{:S(2)}) %collective-permute-start.3) | collective-permute-done | bytes 69664 | tf_op jit(solution)/shard_map/ppermute | solution.py:401
  20.1 0.0 copy-start.4
  20.1 0.0 copy-done.1
  20.1 0.0 copy-done.2
  20.1 0.0 copy-done.3
  20.1 0.6 copy-done.4
  20.8 11.1 %dft.1 = bf16[5120,128]{1,0:T(8,128)(2,1)} custom-call(bf16[272,128]{1,0:T(8,128)(2,1)} %copy-done.1, bf16[272,128]{1,0:T(8,128)(2,1)} %copy-done.2, bf16[272,128]{1,0:T(8,128)(2,1)} %copy-done.3, bf16[272,128]{1,0:T(8,128)(2,1)} %copy-done.4, s32[10,128]{1,0:T(8,128)} %bitcast.11, bf16[22,256,128]{2,1,0:T(8,128)(2,1)} %ready.1.rows, ...), custom_call_target="tpu_custom_call" | custom-call | flops 4294967296 | bytes 16777216 | tf_op jit(solution)/shard_map/dft/pallas_call | solution.py:210
  31.8 9.4 %all-to-all-start = ((bf16[256,5,4,128]{3,2,1,0:T(4,128)(2,1)}), bf16[256,5,4,128]{3,2,1,0:T(4,128)(2,1)S(1)}, u32[]{:S(2)}, u32[]{:S(2)}) async-start(bf16[256,5,4,128]{3,2,1,0:T(4,128)(2,1)} %bitcast.8), calls=%async_computation | async-start | bytes 2621440 | tf_op jit(solution)/shard_map/all_to_all | solution.py:405
  41.2 7.3 %prepare.1 = (bf16[256,256]{1,0:T(8,128)(2,1)}, bf16[512,512]{1,0:T(8,128)(2,1)}, f32[256,1280]{1,0:T(8,128)}, bf16[5,256,1280]{2,1,0:T(8,128)(2,1)}) custom-call(f32[64,64]{1,0:T(8,128)} %modes.1, f32[64,64]{1,0:T(8,128)} %back.1, f32[1,64]{1,0:T(1,128)} %bitcast.12, bf16[5,256,1280]{2,1,0:T(8,128)(2,1)} %legendre), custom_call_target="tpu_custom_call" | custom-call | flops 2147483648 | bytes 8388608 | tf_op jit(solution)/shard_map/prepare/pallas_call | solution.py:270
  48.5 29.4 %all-to-all-done = bf16[256,5,4,128]{3,2,1,0:T(4,128)(2,1)S(1)} async-done(((bf16[256,5,4,128]{3,2,1,0:T(4,128)(2,1)}), bf16[256,5,4,128]{3,2,1,0:T(4,128)(2,1)S(1)}, u32[]{:S(2)}, u32[]{:S(2)}) %all-to-all-start) | async-done | bytes 1310752 | tf_op jit(solution)/shard_map/all_to_all | solution.py:405
  77.9 0.0 copy-start
  77.9 1.1 %copy-done = bf16[256,5,4,128]{3,2,1,0:T(4,128)(2,1)} copy-done((bf16[256,5,4,128]{3,2,1,0:T(4,128)(2,1)}, bf16[256,5,4,128]{3,2,1,0:T(4,128)(2,1)S(1)}, u32[]{:S(2)}) %copy-start) | copy-done | bytes 1310744
  79.0 11.4 %receive.1 = bf16[1280,2,1280]{2,1,0:T(2,128)(2,1)} custom-call(s32[1280]{0:T(1024)} %waves.1, bf16[5120,128]{1,0:T(8,128)(2,1)} %bitcast.9, bf16[5,256,1280]{2,1,0:T(8,128)(2,1)} %get-tuple-element.21.legendre, bf16[256,256]{1,0:T(8,128)(2,1)} %get-tuple-element.22.ahead, bf16[512,512]{1,0:T(8,128)(2,1)} %get-tuple-element.23.behind, ...), custom_call_target="tpu_custom_call" | custom-call | flops 6442450944 | bytes 14680064 | tf_op jit(solution)/shard_map/receive/pallas_call | solution.py:370
Async XLA Ops:
  2.5 14.2 %collective-permute-start = (bf16[272,128]{1,0:T(8,128)(2,1)}, bf16[272,128]{1,0:T(8,128)(2,1)S(1)}, u32[]{:S(2)}, u32[]{:S(2)}) collective-permute-start(bf16[272,128]{1,0:T(8,128)(2,1)} %get-tuple-element.15), channel_id=1, source_target_pairs={{0,30},{1,31},{2,0},{3,1},{4,2},{5,3},{6,4},{7,5},{8,6},{9,7},{10,... | collective-permute-start | bytes 208904 | tf_op jit(solution)/shard_map/ppermute | solution.py:401
  11.6 5.1 %collective-permute-start.1 = (bf16[272,128]{1,0:T(8,128)(2,1)}, bf16[272,128]{1,0:T(8,128)(2,1)S(1)}, u32[]{:S(2)}, u32[]{:S(2)}) collective-permute-start(bf16[272,128]{1,0:T(8,128)(2,1)} %get-tuple-element.16), channel_id=1, source_target_pairs={{0,31},{1,0},{2,1},{3,2},{4,3},{5,4},{6,5},{7,6},{8,7},{9,8},{10,9... | collective-permute-start | bytes 208904 | tf_op jit(solution)/shard_map/ppermute | solution.py:401
  12.4 6.7 %collective-permute-start.2 = (bf16[272,128]{1,0:T(8,128)(2,1)}, bf16[272,128]{1,0:T(8,128)(2,1)S(1)}, u32[]{:S(2)}, u32[]{:S(2)}) collective-permute-start(bf16[272,128]{1,0:T(8,128)(2,1)} %get-tuple-element.17), channel_id=1, source_target_pairs={{0,1},{1,2},{2,3},{3,4},{4,5},{5,6},{6,7},{7,8},{8,9},{9,10},{10,1... | collective-permute-start | bytes 208904 | tf_op jit(solution)/shard_map/ppermute | solution.py:401
  13.1 7.0 %collective-permute-start.3 = (bf16[272,128]{1,0:T(8,128)(2,1)}, bf16[272,128]{1,0:T(8,128)(2,1)S(1)}, u32[]{:S(2)}, u32[]{:S(2)}) collective-permute-start(bf16[272,128]{1,0:T(8,128)(2,1)} %get-tuple-element.18), channel_id=1, source_target_pairs={{0,2},{1,3},{2,4},{3,5},{4,6},{5,7},{6,8},{7,9},{8,10},{9,11},{10,... | collective-permute-start | bytes 208904 | tf_op jit(solution)/shard_map/ppermute | solution.py:401
  16.7 3.4 %copy-start.1 = (bf16[272,128]{1,0:T(8,128)(2,1)}, bf16[272,128]{1,0:T(8,128)(2,1)S(1)}, u32[]{:S(2)}) copy-start(bf16[272,128]{1,0:T(8,128)(2,1)S(1)} %collective-permute-done.m0) | copy-start | bytes 208900
  16.7 3.4 %copy-start.2 = (bf16[272,128]{1,0:T(8,128)(2,1)}, bf16[272,128]{1,0:T(8,128)(2,1)S(1)}, u32[]{:S(2)}) copy-start(bf16[272,128]{1,0:T(8,128)(2,1)S(1)} %collective-permute-done.1.m1) | copy-start | bytes 208900
  19.1 1.0 %copy-start.3 = (bf16[272,128]{1,0:T(8,128)(2,1)}, bf16[272,128]{1,0:T(8,128)(2,1)S(1)}, u32[]{:S(2)}) copy-start(bf16[272,128]{1,0:T(8,128)(2,1)S(1)} %collective-permute-done.2.m2) | copy-start | bytes 208900
  20.1 0.6 copy-start.4
  31.8 46.1 %all-to-all-start = ((bf16[256,5,4,128]{3,2,1,0:T(4,128)(2,1)}), bf16[256,5,4,128]{3,2,1,0:T(4,128)(2,1)S(1)}, u32[]{:S(2)}, u32[]{:S(2)}) async-start(bf16[256,5,4,128]{3,2,1,0:T(4,128)(2,1)} %bitcast.8), calls=%async_computation | async-start | bytes 2621440 | tf_op jit(solution)/shard_map/all_to_all | solution.py:405
  77.9 1.1 %copy-start = (bf16[256,5,4,128]{3,2,1,0:T(4,128)(2,1)}, bf16[256,5,4,128]{3,2,1,0:T(4,128)(2,1)S(1)}, u32[]{:S(2)}) copy-start(bf16[256,5,4,128]{3,2,1,0:T(4,128)(2,1)S(1)} %all-to-all-done) | copy-start | bytes 3932164

commit v3 on v2

v3 whole, which is shorter than its diff:
```python
import math

import jax
import jax.numpy as jnp
import ml_dtypes
import numpy as np
from jax import lax
from jax.experimental import pallas as pl
from jax.experimental.pallas import tpu as pltpu
from jax.sharding import PartitionSpec as P

MW = 1280
NLON = 2816
F = 4
LEV = 64
BLK = 128
CAP = 8
REACH = 2
SLOTS = 32
NLAT = 256
HALF = NLON // 2
CHUNKS = NLON // BLK
OFFSETS = (-2, -1, 1, 2)
MSG = CAP * 32 + 16
BF = jnp.bfloat16
F32 = jnp.float32

MIB = 1 << 20


def half_table():
    order = np.arange(MW, dtype=np.int64).reshape(MW // 2, 2).T
    phase = order[:, :, None] * np.arange(HALF, dtype=np.int64)[None, None, :] % NLON
    angle = phase.astype(np.float32) * np.float32(2.0 * math.pi / NLON)
    scale = np.float32(1.0 / math.sqrt(NLON))
    both = np.stack([np.cos(angle) * scale, -np.sin(angle) * scale], 1)
    return both.reshape(2, MW, HALF).astype(ml_dtypes.bfloat16)


def dot(a, b):
    return lax.dot_general(a, b, (((1,), (0,)), ((), ())), preferred_element_type=F32)


def dot_nt(a, b):
    return lax.dot_general(a, b, (((1,), (1,)), ((), ())), preferred_element_type=F32)


def pack_kernel(owner, block, count, values, *refs):
    outs = refs[:4]
    owner_s, block_s, count_s, held, lists, used, sems = refs[4:]
    copies = [
        pltpu.make_async_copy(source, target, sems.at[i])
        for i, (source, target) in enumerate(
            ((owner, owner_s), (block, block_s), (count, count_s), (values, held))
        )
    ]
    for copy in copies:
        copy.start()
    band = lax.axis_index("wave")
    for number in range(5):
        used[number] = 0
    for copy in copies[:3]:
        copy.wait()
    for slot in range(SLOTS):
        step = owner_s[0, slot] - band
        number = jnp.where(step < 0, step + REACH, step + REACH - 1)
        number = jnp.where(slot < count_s[0], jnp.clip(number, 0, 4), 4)
        at = used[number]
        lists[number, at] = slot
        used[number] = at + 1
    row = lax.broadcasted_iota(jnp.int32, (16, BLK), 0)
    copies[3].wait()
    for number, out in enumerate(outs):
        marks = jnp.zeros((16, BLK), F32)
        for at in range(CAP):
            valid = at < used[number]
            slot = jnp.where(valid, lists[number, at], 0)
            out[at * 32 : (at + 1) * 32, :] = jnp.where(valid, held[slot], 0.0).astype(BF)
            which = jnp.where(valid, block_s[0, slot], 0).astype(F32)
            marks = jnp.where(row == at, which, marks)
        out[CAP * 32 :, :] = marks.astype(BF)


def params(room, flops=0, read=0):
    return dict(
        compiler_params=pltpu.CompilerParams(vmem_limit_bytes=int(room * MIB)),
        cost_estimate=pl.CostEstimate(flops=flops, bytes_accessed=read, transcendentals=0),
    )


def pack(owner, block, count, values):
    vmem = pl.BlockSpec(memory_space=pltpu.VMEM)
    return pl.pallas_call(
        pack_kernel,
        out_shape=[jax.ShapeDtypeStruct((MSG, BLK), BF)] * 4,
        in_specs=[pl.BlockSpec(memory_space=pl.ANY)] * 4,
        out_specs=[vmem] * 4,
        scratch_shapes=[
            pltpu.SMEM((1, SLOTS), jnp.int32),
            pltpu.SMEM((1, SLOTS), jnp.int32),
            pltpu.SMEM((1,), jnp.int32),
            pltpu.VMEM((SLOTS, 32, BLK), F32),
            pltpu.SMEM((5, SLOTS), jnp.int32),
            pltpu.SMEM((5,), jnp.int32),
            pltpu.SemaphoreType.DMA((4,)),
        ],
        name="pack",
        **params(60, read=1 << 20),
    )(owner, block, count, values)


def ready_kernel(grid, table, made, table_v, held, sems):
    whole = pltpu.make_async_copy(table, table_v, sems.at[2])
    parts = [
        pltpu.make_async_copy(grid.at[pl.ds(16 * i, 16)], held.at[pl.ds(16 * i, 16)], sems.at[i])
        for i in range(2)
    ]
    for part in parts + [whole]:
        part.start()
    for i, part in enumerate(parts):
        part.wait()
        for c in range(CHUNKS):
            block = held[16 * i : 16 * i + 16, :, c * BLK : (c + 1) * BLK].astype(F32)
            block = jnp.swapaxes(block, 0, 1).astype(BF)
            for j in range(8):
                made[c, j * 32 + 16 * i : j * 32 + 16 * i + 16, :] = block[j]
    whole.wait()


def ready(grid, table):
    hbm = pl.BlockSpec(memory_space=pltpu.HBM)
    vmem = pl.BlockSpec(memory_space=pltpu.VMEM)
    return pl.pallas_call(
        ready_kernel,
        out_shape=[
            jax.ShapeDtypeStruct((CHUNKS, 256, BLK), BF),
            jax.ShapeDtypeStruct(table.shape, BF),
        ],
        in_specs=[hbm, hbm],
        out_specs=[vmem, vmem],
        scratch_shapes=[
            pltpu.VMEM((32, 8, NLON), BF),
            pltpu.SemaphoreType.DMA((3,)),
        ],
        name="ready",
        **params(46, read=10 << 20),
    )(grid, table)


def dft_kernel(
    m0, m1, m2, m3, waves, raw, even, odd, out, acc, pick, surf, four, strided, marks, marks_s, sem
):
    messages = (m0, m1, m2, m3)
    for number, message in enumerate(messages):
        marks[pl.ds(number * CAP, CAP), :] = (
            message[pl.ds(CAP * 32, 16), :].astype(F32)[:CAP].astype(jnp.int32)
        )
    to_scalar = pltpu.make_async_copy(marks, marks_s, sem)
    to_scalar.start()
    acc[...] = raw[...].astype(F32)
    to_scalar.wait()
    for number, message in enumerate(messages):
        for r in range(CAP):
            b = marks_s[number * CAP + r, 0]
            j = b // CHUNKS
            c = b - j * CHUNKS
            at = pl.ds(pl.multiple_of(j * 32, 32), 32)
            acc[c, at, :] = acc[c, at, :] + message[pl.ds(r * 32, 32), :].astype(F32)
    for c in range(CHUNKS // 2):
        near, far = acc[c], acc[c + CHUNKS // 2]
        surf[0, :, c * BLK : (c + 1) * BLK] = (near + far).astype(BF)
        surf[1, :, c * BLK : (c + 1) * BLK] = (near - far).astype(BF)
    half = MW // 2
    column = lax.broadcasted_iota(jnp.int32, (BLK, BLK), 1)
    for p, table in enumerate((even, odd)):
        both = dot_nt(table[...], surf[p]).astype(BF)
        for b in range(p * 5, p * 5 + 5):
            m = waves[b : b + 1, :]
            key = (m % 2) * half + m // 2
            key = jnp.broadcast_to(key.astype(F32), (BLK, BLK)).T.astype(jnp.int32)
            for t in range(MW // BLK):
                pick[b * BLK : (b + 1) * BLK, t * BLK : (t + 1) * BLK] = jnp.where(
                    key == column + t * BLK, 1.0, 0.0
                ).astype(BF)
        for part in range(2):
            four[p * half : (p + 1) * half, part * 256 : (part + 1) * 256] = both[
                part * half : (part + 1) * half
            ]
    for b in range(2):
        found = dot(pick[b * half : (b + 1) * half], four[...])
        for q in range(4):
            strided[b, pl.ds(q, half, stride=4), :] = found[:, q * BLK : (q + 1) * BLK]
        out[b * 4 * half : (b + 1) * 4 * half, :] = strided[b].astype(BF)


def dft(messages, waves, rows, even, odd):
    vmem = pl.BlockSpec(memory_space=pltpu.VMEM)
    return pl.pallas_call(
        dft_kernel,
        out_shape=jax.ShapeDtypeStruct((MW * 4, BLK), BF),
        in_specs=[vmem] * 8,
        out_specs=vmem,
        scratch_shapes=[
            pltpu.VMEM((CHUNKS, 256, BLK), F32),
            pltpu.VMEM((MW, MW), BF),
            pltpu.VMEM((2, 256, HALF), BF),
            pltpu.VMEM((MW, 512), BF),
            pltpu.VMEM((2, MW * 2, BLK), F32),
            pltpu.VMEM((SLOTS, BLK), jnp.int32),
            pltpu.SMEM((SLOTS, BLK), jnp.int32),
            pltpu.SemaphoreType.DMA,
        ],
        name="dft",
        **params(44, flops=4 << 30, read=16 << 20),
    )(*messages, waves, rows, even, odd)


def prepare_kernel(modes, back, eigen, legendre, ahead, behind, scale, turned, held, sems):
    copies = [pltpu.make_async_copy(legendre.at[s], held.at[s], sems.at[s]) for s in range(5)]
    for copy in copies:
        copy.start()
    row = lax.broadcasted_iota(jnp.int32, (256, 256), 0)
    place = lax.rem(row, 32) * 8 + lax.rem(row // 32, 2) * 4 + row // 64
    move = jnp.where(place == lax.broadcasted_iota(jnp.int32, (256, 256), 1), 1.0, 0.0)
    spread = jnp.where(
        lax.broadcasted_iota(jnp.int32, (256, LEV), 0) // F
        == lax.broadcasted_iota(jnp.int32, (256, LEV), 1),
        1.0,
        0.0,
    )
    picks = spread.astype(BF)
    row = lax.broadcasted_iota(jnp.int32, (256, 256), 0)
    column = lax.broadcasted_iota(jnp.int32, (256, 256), 1)
    same = lax.rem(row, F) == lax.rem(column, F)
    rows = dot_nt(picks, modes[...].astype(BF)).astype(BF)
    ahead[...] = jnp.where(same, dot_nt(rows, picks), 0.0).astype(BF)
    rows = dot_nt(picks, back[...].astype(BF)).astype(BF)
    single = jnp.where(same, dot_nt(rows, picks), 0.0).astype(BF)
    row = lax.broadcasted_iota(jnp.int32, (512, 256), 0)
    column = lax.broadcasted_iota(jnp.int32, (512, 256), 1)
    for part in range(2):
        chosen = jnp.where(row == column * 2 + part, 1.0, 0.0).astype(BF)
        behind[:, part * 256 : (part + 1) * 256] = dot(chosen, single).astype(BF)
    value = jnp.sum(spread * eigen[...], axis=1, keepdims=True)
    order = lax.broadcasted_iota(jnp.int32, (1, MW), 1).astype(F32)
    ratio = order * (order + 1.0) / (MW * (MW - 1.0))
    scale[...] = 1.0 / (1.0 + value * ratio)
    for s, copy in enumerate(copies):
        copy.wait()
        turned[s] = dot(move.astype(BF), held[s]).astype(BF)


def prepare(modes, back, eigen, legendre):
    vmem = pl.BlockSpec(memory_space=pltpu.VMEM)
    return pl.pallas_call(
        prepare_kernel,
        out_shape=[
            jax.ShapeDtypeStruct((256, 256), BF),
            jax.ShapeDtypeStruct((512, 512), BF),
            jax.ShapeDtypeStruct((256, MW), F32),
            jax.ShapeDtypeStruct((5, NLAT, MW), BF),
        ],
        in_specs=[vmem] * 3 + [pl.BlockSpec(memory_space=pltpu.HBM)],
        out_specs=[vmem] * 4,
        scratch_shapes=[pltpu.VMEM((5, NLAT, MW), BF), pltpu.SemaphoreType.DMA((5,))],
        name="prepare",
        **params(16, flops=2 << 30, read=8 << 20),
    )(modes, back, eigen, legendre)


def receive_kernel(
    waves, moved, legendre, ahead, behind, scale, out, spread, latitude, projected, made, tables, sems, sems_out
):
    copies = [pltpu.make_async_copy(legendre.at[s], tables.at[s], sems.at[s]) for s in range(5)]
    for copy in copies:
        copy.start()
    for j in range(4):
        for lanes in range(2):
            mixed = jnp.concatenate(
                [
                    moved[lev * 640 : (lev + 1) * 640, j * 32 : (j + 1) * 32]
                    for lev in range(lanes * 4, lanes * 4 + 4)
                ],
                1,
            )
            spread[j, lanes] = mixed.astype(F32)

    def gather(s):
        for part in range(2):
            for j in range(4):
                for jq in range(2):
                    for lanes in range(2):
                        at = part * 256 + j * 64 + jq * 32
                        latitude[s, at : at + 32, lanes * BLK : (lanes + 1) * BLK] = spread[
                            j, lanes, pl.ds((2 * s + part) * 2 + jq, 32, stride=20), :
                        ].astype(BF)

    def project(s):
        projected[s] = dot_nt(ahead[...], latitude[s]).astype(BF)

    gather(0)
    project(0)
    first = (lax.axis_index("lev") * 32 + lax.axis_index("wave")) * 5
    order = lax.broadcasted_iota(jnp.int32, (1, MW), 1)
    sends = []
    for s in range(5):
        copies[s].wait()
        if s < 4:
            gather(s + 1)
        factor = jnp.where(order >= waves[first + s], scale[...], 0.0)
        scaled = [
            (dot(projected[s, :, part * 256 : (part + 1) * 256], tables[s]) * factor).astype(BF)
            for part in range(2)
        ]
        made.at[s].reshape(512, MW)[...] = dot(behind[...], jnp.concatenate(scaled, 0)).astype(BF)
        send = pltpu.make_async_copy(made.at[s], out.at[pl.ds(s * 256, 256)], sems_out.at[s])
        send.start()
        sends.append(send)
        if s < 4:
            project(s + 1)
    for send in sends:
        send.wait()


def receive(waves, moved, legendre, ahead, behind, scale):
    hbm = pl.BlockSpec(memory_space=pl.ANY)
    return pl.pallas_call(
        receive_kernel,
        out_shape=jax.ShapeDtypeStruct((5 * 256, 2, MW), BF),
        in_specs=[pl.BlockSpec(memory_space=pltpu.SMEM)]
        + [pl.BlockSpec(memory_space=pltpu.VMEM)]
        + [hbm]
        + [pl.BlockSpec(memory_space=pltpu.VMEM)] * 3,
        out_specs=hbm,
        scratch_shapes=[
            pltpu.VMEM((4, 2, 640, BLK), F32),
            pltpu.VMEM((5, 512, 256), BF),
            pltpu.VMEM((5, 256, 512), BF),
            pltpu.VMEM((5, 256, 2, MW), BF),
            pltpu.VMEM((5, NLAT, MW), BF),
            pltpu.SemaphoreType.DMA((5,)),
            pltpu.SemaphoreType.DMA((5,)),
        ],
        name="receive",
        **params(48, flops=6 << 30, read=14 << 20),
    )(waves, moved, legendre, ahead, behind, scale)


def shards(
    even, odd, grid, halo_values, halo_owner, halo_block, halo_count, wave_list, legendre, modes, back, eigen
):
    bands = lax.axis_size("wave")
    sent = pack(halo_owner, halo_block, halo_count, halo_values.reshape(SLOTS, 32, BLK))
    came = []
    for message, step in zip(sent, OFFSETS):
        route = [(i, (i + step) % bands) for i in range(bands)]
        came.append(lax.ppermute(message, "wave", route))
    grid, _ = lax.optimization_barrier((grid, sent))
    rows, even = ready(grid.reshape(32, 8, NLON), even)
    fourier = dft(came, wave_list.reshape(10, BLK), rows, even, odd)
    moved = lax.all_to_all(
        fourier.reshape(256, 5, 4, BLK), ("lev", "wave"), split_axis=0, concat_axis=0, tiled=True
    ).reshape(5120, BLK)
    legendre, _ = lax.optimization_barrier((legendre, fourier))
    ahead, behind, scale, turned = prepare(modes, back, eigen.reshape(1, LEV), legendre)
    result = receive(wave_list, moved, turned, ahead, behind, scale)
    return result.reshape(5, LEV, F, 2, MW)


def solution(mesh):
    placed = (
        P("lev", None, "wave", None),
        P("wave", None, "lev", None, None),
        P("wave", None),
        P("wave", None),
        P("wave"),
        P(),
        P(("lev", "wave"), None, None),
        P(),
        P(),
        P(),
    )
    mapped = jax.shard_map(
        shards,
        mesh=mesh,
        in_specs=(P(), P()) + placed,
        out_specs=P(("lev", "wave"), None, None, None, None),
        check_vma=False,
    )
    table = half_table()

    def whole(*args):
        return mapped(jnp.asarray(table[0]), jnp.asarray(table[1]), *args)

    return whole
```

time: 91 us -> 83.4 us (0.916)
  Pallas kernels: 34.5 us -> 25.1 us
  local copies, waits for them, and re-layouts: 1.7 us -> 4.97 us
  waiting for transfers between devices: 32.8 us -> 31.4 us
    pallas_call x1, Pallas kernels: 11.1 us -> 6.47 us  [dft(): pl.pallas_call(dft_kernel, out_shape=jax.ShapeDtypeStruct((MW * 4, BLK),...]
    pallas_call x2, Pallas kernels: 10.1 us -> 6.54 us  [the longest x1 3.65 us: prepare(): pl.pallas_call(prepare_kernel, out_shape=[jax.ShapeDtypeStruct((256, 256)...]
    unnamed x10 -> x16, local copies, waits for them, and re-layouts: 1.7 us -> 4.97 us
    ppermute x4, waiting for transfers between devices: 3.39 us -> 2.01 us  [shards(): came.append(lax.ppermute(message, 'wave', route))]
    pallas_call x1, Pallas kernels: 11.4 us -> 10.2 us  [receive(): pl.pallas_call(receive_kernel, out_shape=jax.ShapeDtypeStruct((5 * 256, 2...]
  transfers between devices with their start and end apart: 5 -> 5, of which waited for: 3 -> 3; matrix products, arithmetic and copies ran while one was open for 0% -> 0% of each run, Pallas kernels for 11% -> 8%
where the time goes in v3:
time: 83.4 us; the launch traced here: 83.1 us
  waiting for transfers between devices  31.4 us (38%)
  Pallas kernels  25.1 us (30%)
  starting transfers between devices  20.7 us (25%)
  local copies, waits for them, and re-layouts  4.97 us (6%)
  between operations  0.94 us (1%)
    all_to_all x1, waiting for transfers between devices, shards(): lax.all_to_all(fourier.reshape(256, 5, 4, BLK), ('lev', 'wave'), split_ax...  29.4 us
    ppermute x4, starting transfers between devices, shards(): came.append(lax.ppermute(message, 'wave', route))  11.3 us
    pallas_call x1, Pallas kernels, receive(): pl.pallas_call(receive_kernel, out_shape=jax.ShapeDtypeStruct((5 * 256, 2...  10.2 us
    all_to_all x1, starting transfers between devices, shards(): lax.all_to_all(fourier.reshape(256, 5, 4, BLK), ('lev', 'wave'), split_ax...  9.35 us
    pallas_call x1, Pallas kernels, dft(): pl.pallas_call(dft_kernel, out_shape=jax.ShapeDtypeStruct((MW * 4, BLK),...  6.47 us
    unnamed x16, local copies, waits for them, and re-layouts  4.97 us
    pallas_call x1, Pallas kernels, prepare(): pl.pallas_call(prepare_kernel, out_shape=[jax.ShapeDtypeStruct((256, 256)...  3.65 us
    pallas_call x1, Pallas kernels, ready(): pl.pallas_call(ready_kernel, out_shape=[jax.ShapeDtypeStruct((CHUNKS, 256...  2.9 us
  transfers between devices with their start and end apart: 5, of which 3 were waited for; matrix products, arithmetic and copies ran while one was open for 0% of the time, Pallas kernels for 8%

profile of v3, /device:TPU:1, one launch (start us, length us, event | category | flops | bytes accessed | tf_op | source)
XLA Modules:
  0.0 83.1 jit_solution(3675623382425654950)
XLA Ops:
  0.0 0.0 copy-start.4
  0.7 1.9 %pack.1 = (bf16[272,128]{1,0:T(8,128)(2,1)}, bf16[272,128]{1,0:T(8,128)(2,1)}, bf16[272,128]{1,0:T(8,128)(2,1)}, bf16[272,128]{1,0:T(8,128)(2,1)}) custom-call(s32[1,32]{1,0:T(1,128)} %owner.1, s32[1,32]{1,0:T(1,128)} %block.1, s32[1]{0:T(128)S(6)} %copy.13.count, f32[32,32,128]{2,1,0:T(8,128)} %bitcast.11), custom_call_target="tpu_custom_call" | custom-call | bytes 1048576 | tf_op jit(solution)/shard_map/pack/pallas_call | solution.py:93
  2.5 9.1 %collective-permute-start = (bf16[272,128]{1,0:T(8,128)(2,1)}, bf16[272,128]{1,0:T(8,128)(2,1)S(1)}, u32[]{:S(2)}, u32[]{:S(2)}) collective-permute-start(bf16[272,128]{1,0:T(8,128)(2,1)} %get-tuple-element.17), channel_id=1, source_target_pairs={{0,30},{1,31},{2,0},{3,1},{4,2},{5,3},{6,4},{7,5},{8,6},{9,7},{10,... | collective-permute-start | bytes 208904 | tf_op jit(solution)/shard_map/ppermute | solution.py:357
  11.7 0.8 collective-permute-start.1
  12.4 0.7 collective-permute-start.2
  13.1 0.7 collective-permute-start.3
  13.8 0.0 copy-start
  13.8 1.4 %copy-done = bf16[8,4,8,2816]{3,2,1,0:T(8,128)(2,1)S(1)} copy-done((bf16[8,4,8,2816]{3,2,1,0:T(8,128)(2,1)S(1)}, bf16[8,4,8,2816]{3,2,1,0:T(8,128)(2,1)}, u32[]{:S(2)}) %copy-start) | copy-done | bytes 1441816
  15.2 0.0 copy-start.6
  15.2 2.9 %ready.1 = (bf16[22,256,128]{2,1,0:T(8,128)(2,1)S(1)}, bf16[1280,1408]{1,0:T(8,128)(2,1)S(1)}) custom-call(bf16[32,8,2816]{2,1,0:T(8,128)(2,1)S(1)} %bitcast.7, bf16[1280,1408]{1,0:T(8,128)(2,1)} %constant.4.clone.table), custom_call_target="tpu_custom_call" | custom-call | bytes 10485760 | tf_op jit(solution)/shard_map/ready/pallas_call | solution.py:133
  18.1 0.0 collective-permute-done.m0
  18.1 0.0 collective-permute-done.1.m1
  18.1 1.0 %collective-permute-done.2.m2 = bf16[272,128]{1,0:T(8,128)(2,1)S(1)} collective-permute-done((bf16[272,128]{1,0:T(8,128)(2,1)}, bf16[272,128]{1,0:T(8,128)(2,1)S(1)}, u32[]{:S(2)}, u32[]{:S(2)}) %collective-permute-start.2) | collective-permute-done | bytes 69664 | tf_op jit(solution)/shard_map/ppermute | solution.py:357
  19.1 1.0 %collective-permute-done.3.m3 = bf16[272,128]{1,0:T(8,128)(2,1)S(1)} collective-permute-done((bf16[272,128]{1,0:T(8,128)(2,1)}, bf16[272,128]{1,0:T(8,128)(2,1)S(1)}, u32[]{:S(2)}, u32[]{:S(2)}) %collective-permute-start.3) | collective-permute-done | bytes 69664 | tf_op jit(solution)/shard_map/ppermute | solution.py:357
  20.1 0.0 copy-done.4
  20.1 0.0 copy-done.6
  20.1 0.0 copy-start.2
  20.1 0.0 copy-start.3
  20.2 0.0 copy-start.5
  20.2 6.5 %dft.1 = bf16[5120,128]{1,0:T(8,128)(2,1)} custom-call(bf16[272,128]{1,0:T(8,128)(2,1)S(1)} %collective-permute-done.m0, bf16[272,128]{1,0:T(8,128)(2,1)S(1)} %collective-permute-done.1.m1, bf16[272,128]{1,0:T(8,128)(2,1)S(1)} %collective-permute-done.2.m2, bf16[272,128]{1,0:T(8,128)(2,1)S(1)} %collective-permute-done.3.m3, s32[10,128]{1,0:T(8,128)S(1)} %bitcast.9, ...), custom_call_target="tpu_custom_call" | custom-call | flops 4294967296 | bytes 16777216 | tf_op jit(solution)/shard_map/dft/pallas_call | solution.py:198
  26.6 9.4 %all-to-all-start = ((bf16[256,5,4,128]{3,2,1,0:T(4,128)(2,1)}), bf16[256,5,4,128]{3,2,1,0:T(4,128)(2,1)S(1)}, u32[]{:S(2)}, u32[]{:S(2)}) async-start(bf16[256,5,4,128]{3,2,1,0:T(4,128)(2,1)} %bitcast.3), calls=%async_computation | async-start | bytes 2621440 | tf_op jit(solution)/shard_map/all_to_all | solution.py:361
  36.0 0.0 copy-done.2
  36.0 0.0 copy-done.3
  36.0 0.0 copy-done.5
  36.0 0.0 copy-start.1
  36.0 1.9 %copy-done.1 = bf16[5,256,1280]{2,1,0:T(8,128)(2,1)S(1)} copy-done((bf16[5,256,1280]{2,1,0:T(8,128)(2,1)S(1)}, bf16[5,256,1280]{2,1,0:T(8,128)(2,1)}, u32[]{:S(2)}) %copy-start.1) | copy-done | bytes 3276824
  38.0 3.6 %prepare.1 = (bf16[256,256]{1,0:T(8,128)(2,1)S(1)}, bf16[512,512]{1,0:T(8,128)(2,1)S(1)}, f32[256,1280]{1,0:T(8,128)S(1)}, bf16[5,256,1280]{2,1,0:T(8,128)(2,1)S(1)}) custom-call(f32[64,64]{1,0:T(8,128)S(1)} %copy-done.2, f32[64,64]{1,0:T(8,128)S(1)} %copy-done.3, f32[1,64]{1,0:T(1,128)S(1)} %bitcast.10, bf16[5,256,1280]{2,1,0:T(8,128)(2,1)S(1)} %copy-done.1), custom_call_target="tpu_custom_call" | custom-call | flops 2147483648 | bytes 8388608 | tf_op jit(solution)/shard_map/prepare/pallas_call | solution.py:255
  41.6 0.0 copy-start.7
  41.6 1.7 %copy-done.7 = bf16[5,256,1280]{2,1,0:T(8,128)(2,1)} copy-done((bf16[5,256,1280]{2,1,0:T(8,128)(2,1)}, bf16[5,256,1280]{2,1,0:T(8,128)(2,1)S(1)}, u32[]{:S(2)}) %copy-start.7) | copy-done | bytes 3276824
  43.3 29.4 %all-to-all-done = bf16[256,5,4,128]{3,2,1,0:T(4,128)(2,1)S(1)} async-done(((bf16[256,5,4,128]{3,2,1,0:T(4,128)(2,1)}), bf16[256,5,4,128]{3,2,1,0:T(4,128)(2,1)S(1)}, u32[]{:S(2)}, u32[]{:S(2)}) %all-to-all-start) | async-done | bytes 1310752 | tf_op jit(solution)/shard_map/all_to_all | solution.py:361
  72.7 10.2 %receive.1 = bf16[1280,2,1280]{2,1,0:T(2,128)(2,1)} custom-call(s32[1280]{0:T(1024)S(1)} %copy-done.4, bf16[5120,128]{1,0:T(8,128)(2,1)S(1)} %bitcast.8, bf16[5,256,1280]{2,1,0:T(8,128)(2,1)} %copy-done.7, bf16[256,256]{1,0:T(8,128)(2,1)S(1)} %get-tuple-element.26.ahead, bf16[512,512]{1,0:T(8,128)(2,1)S(1)} %get-tuple-element.27.behind, ...), custom_call_target="tpu_custom_call" | custom-call | flops 6442450944 | bytes 14680064 | tf_op jit(solution)/shard_map/receive/pallas_call | solution.py:327
Async XLA Ops:
  0.0 20.1 %copy-start.4 = (s32[1280]{0:T(1024)S(1)}, s32[1280]{0:T(1024)}, u32[]{:S(2)}) copy-start(s32[1280]{0:T(1024)} %waves.1) | copy-start | bytes 15364
  2.5 15.6 %collective-permute-start = (bf16[272,128]{1,0:T(8,128)(2,1)}, bf16[272,128]{1,0:T(8,128)(2,1)S(1)}, u32[]{:S(2)}, u32[]{:S(2)}) collective-permute-start(bf16[272,128]{1,0:T(8,128)(2,1)} %get-tuple-element.17), channel_id=1, source_target_pairs={{0,30},{1,31},{2,0},{3,1},{4,2},{5,3},{6,4},{7,5},{8,6},{9,7},{10,... | collective-permute-start | bytes 208904 | tf_op jit(solution)/shard_map/ppermute | solution.py:357
  11.7 6.5 %collective-permute-start.1 = (bf16[272,128]{1,0:T(8,128)(2,1)}, bf16[272,128]{1,0:T(8,128)(2,1)S(1)}, u32[]{:S(2)}, u32[]{:S(2)}) collective-permute-start(bf16[272,128]{1,0:T(8,128)(2,1)} %get-tuple-element.18), channel_id=1, source_target_pairs={{0,31},{1,0},{2,1},{3,2},{4,3},{5,4},{6,5},{7,6},{8,7},{9,8},{10,9... | collective-permute-start | bytes 208904 | tf_op jit(solution)/shard_map/ppermute | solution.py:357
  12.4 6.7 %collective-permute-start.2 = (bf16[272,128]{1,0:T(8,128)(2,1)}, bf16[272,128]{1,0:T(8,128)(2,1)S(1)}, u32[]{:S(2)}, u32[]{:S(2)}) collective-permute-start(bf16[272,128]{1,0:T(8,128)(2,1)} %get-tuple-element.19), channel_id=1, source_target_pairs={{0,1},{1,2},{2,3},{3,4},{4,5},{5,6},{6,7},{7,8},{8,9},{9,10},{10,1... | collective-permute-start | bytes 208904 | tf_op jit(solution)/shard_map/ppermute | solution.py:357
  13.1 7.0 %collective-permute-start.3 = (bf16[272,128]{1,0:T(8,128)(2,1)}, bf16[272,128]{1,0:T(8,128)(2,1)S(1)}, u32[]{:S(2)}, u32[]{:S(2)}) collective-permute-start(bf16[272,128]{1,0:T(8,128)(2,1)} %get-tuple-element.20), channel_id=1, source_target_pairs={{0,2},{1,3},{2,4},{3,5},{4,6},{5,7},{6,8},{7,9},{8,10},{9,11},{10,... | collective-permute-start | bytes 208904 | tf_op jit(solution)/shard_map/ppermute | solution.py:357
  13.8 1.4 %copy-start = (bf16[8,4,8,2816]{3,2,1,0:T(8,128)(2,1)S(1)}, bf16[8,4,8,2816]{3,2,1,0:T(8,128)(2,1)}, u32[]{:S(2)}) copy-start(bf16[8,4,8,2816]{3,2,1,0:T(8,128)(2,1)} %param.12) | copy-start | bytes 4325380
  15.2 4.9 %copy-start.6 = (bf16[1280,1408]{1,0:T(8,128)(2,1)S(1)}, bf16[1280,1408]{1,0:T(8,128)(2,1)}, u32[]{:S(2)}) copy-start(bf16[1280,1408]{1,0:T(8,128)(2,1)} %constant.5.clone.odd) | copy-start | bytes 10813444
  20.1 15.9 %copy-start.2 = (f32[64,64]{1,0:T(8,128)S(1)}, f32[64,64]{1,0:T(8,128)}, u32[]{:S(2)}) copy-start(f32[64,64]{1,0:T(8,128)} %modes.1) | copy-start | bytes 49156
  20.1 15.9 %copy-start.3 = (f32[64,64]{1,0:T(8,128)S(1)}, f32[64,64]{1,0:T(8,128)}, u32[]{:S(2)}) copy-start(f32[64,64]{1,0:T(8,128)} %back.1) | copy-start | bytes 49156
  20.2 15.9 %copy-start.5 = (f32[64]{0:T(128)S(1)}, f32[64]{0:T(128)}, u32[]{:S(2)}) copy-start(f32[64]{0:T(128)} %param.21) | copy-start | bytes 772
  26.6 46.1 %all-to-all-start = ((bf16[256,5,4,128]{3,2,1,0:T(4,128)(2,1)}), bf16[256,5,4,128]{3,2,1,0:T(4,128)(2,1)S(1)}, u32[]{:S(2)}, u32[]{:S(2)}) async-start(bf16[256,5,4,128]{3,2,1,0:T(4,128)(2,1)} %bitcast.3), calls=%async_computation | async-start | bytes 2621440 | tf_op jit(solution)/shard_map/all_to_all | solution.py:361
  36.0 1.9 %copy-start.1 = (bf16[5,256,1280]{2,1,0:T(8,128)(2,1)S(1)}, bf16[5,256,1280]{2,1,0:T(8,128)(2,1)}, u32[]{:S(2)}) copy-start(bf16[5,256,1280]{2,1,0:T(8,128)(2,1)} %legendre) | copy-start | bytes 9830404
  41.6 1.7 %copy-start.7 = (bf16[5,256,1280]{2,1,0:T(8,128)(2,1)}, bf16[5,256,1280]{2,1,0:T(8,128)(2,1)S(1)}, u32[]{:S(2)}) copy-start(bf16[5,256,1280]{2,1,0:T(8,128)(2,1)S(1)} %get-tuple-element.25.legendre) | copy-start | bytes 9830404

commit v4 on v3

--- a/solution.py
+++ b/solution.py
@@ -15,6 +15,7 @@
 LEV = 64
 BLK = 128
 CAP = 8
+SENDS = 4
 REACH = 2
 SLOTS = 32
 NLAT = 256
@@ -109,18 +110,12 @@
     )(owner, block, count, values)
 
 
-def ready_kernel(grid, table, made, table_v, held, sems):
-    whole = pltpu.make_async_copy(table, table_v, sems.at[2])
-    parts = [
-        pltpu.make_async_copy(grid.at[pl.ds(16 * i, 16)], held.at[pl.ds(16 * i, 16)], sems.at[i])
-        for i in range(2)
-    ]
-    for part in parts + [whole]:
-        part.start()
-    for i, part in enumerate(parts):
-        part.wait()
+def ready_kernel(grid, table, made, table_v, sem):
+    whole = pltpu.make_async_copy(table, table_v, sem)
+    whole.start()
+    for i in range(2):
         for c in range(CHUNKS):
-            block = held[16 * i : 16 * i + 16, :, c * BLK : (c + 1) * BLK].astype(F32)
+            block = grid[16 * i : 16 * i + 16, :, c * BLK : (c + 1) * BLK].astype(F32)
             block = jnp.swapaxes(block, 0, 1).astype(BF)
             for j in range(8):
                 made[c, j * 32 + 16 * i : j * 32 + 16 * i + 16, :] = block[j]
@@ -136,19 +131,16 @@
             jax.ShapeDtypeStruct((CHUNKS, 256, BLK), BF),
             jax.ShapeDtypeStruct(table.shape, BF),
         ],
-        in_specs=[hbm, hbm],
+        in_specs=[vmem, hbm],
         out_specs=[vmem, vmem],
-        scratch_shapes=[
-            pltpu.VMEM((32, 8, NLON), BF),
-            pltpu.SemaphoreType.DMA((3,)),
-        ],
+        scratch_shapes=[pltpu.SemaphoreType.DMA],
         name="ready",
         **params(46, read=10 << 20),
     )(grid, table)
 
 
 def dft_kernel(
-    m0, m1, m2, m3, waves, raw, even, odd, out, acc, pick, surf, four, strided, marks, marks_s, sem
+    m0, m1, m2, m3, waves, raw, even, odd, out, acc, pick, surf, four, strided, leaving, marks, marks_s, sem, sems
 ):
     messages = (m0, m1, m2, m3)
     for number, message in enumerate(messages):
@@ -173,7 +165,6 @@
     half = MW // 2
     column = lax.broadcasted_iota(jnp.int32, (BLK, BLK), 1)
     for p, table in enumerate((even, odd)):
-        both = dot_nt(table[...], surf[p]).astype(BF)
         for b in range(p * 5, p * 5 + 5):
             m = waves[b : b + 1, :]
             key = (m % 2) * half + m // 2
@@ -182,15 +173,24 @@
                 pick[b * BLK : (b + 1) * BLK, t * BLK : (t + 1) * BLK] = jnp.where(
                     key == column + t * BLK, 1.0, 0.0
                 ).astype(BF)
+        both = dot_nt(table[...], surf[p]).astype(BF)
         for part in range(2):
             four[p * half : (p + 1) * half, part * 256 : (part + 1) * 256] = both[
                 part * half : (part + 1) * half
             ]
-    for b in range(2):
-        found = dot(pick[b * half : (b + 1) * half], four[...])
+    slots = MW // SENDS
+    sends = []
+    for b in range(SENDS):
+        found = dot(pick[b * slots : (b + 1) * slots], four[...])
         for q in range(4):
-            strided[b, pl.ds(q, half, stride=4), :] = found[:, q * BLK : (q + 1) * BLK]
-        out[b * 4 * half : (b + 1) * 4 * half, :] = strided[b].astype(BF)
+            strided[b, pl.ds(q, slots, stride=4), :] = found[:, q * BLK : (q + 1) * BLK]
+        rows = pl.ds(b * 4 * slots, 4 * slots)
+        leaving[rows, :] = strided[b].astype(BF)
+        send = pltpu.make_async_copy(leaving.at[rows], out.at[rows], sems.at[b])
+        send.start()
+        sends.append(send)
+    for send in sends:
+        send.wait()
 
 
 def dft(messages, waves, rows, even, odd):
@@ -199,16 +199,18 @@
         dft_kernel,
         out_shape=jax.ShapeDtypeStruct((MW * 4, BLK), BF),
         in_specs=[vmem] * 8,
-        out_specs=vmem,
+        out_specs=pl.BlockSpec(memory_space=pl.ANY),
         scratch_shapes=[
             pltpu.VMEM((CHUNKS, 256, BLK), F32),
             pltpu.VMEM((MW, MW), BF),
             pltpu.VMEM((2, 256, HALF), BF),
             pltpu.VMEM((MW, 512), BF),
-            pltpu.VMEM((2, MW * 2, BLK), F32),
+            pltpu.VMEM((SENDS, MW * 4 // SENDS, BLK), F32),
+            pltpu.VMEM((MW * 4, BLK), BF),
             pltpu.VMEM((SLOTS, BLK), jnp.int32),
             pltpu.SMEM((SLOTS, BLK), jnp.int32),
             pltpu.SemaphoreType.DMA,
+            pltpu.SemaphoreType.DMA((SENDS,)),
         ],
         name="dft",
         **params(44, flops=4 << 30, read=16 << 20),
@@ -303,7 +305,7 @@
     first = (lax.axis_index("lev") * 32 + lax.axis_index("wave")) * 5
     order = lax.broadcasted_iota(jnp.int32, (1, MW), 1)
     sends = []
-    for s in range(5):
+    def work(s, send):
         copies[s].wait()
         if s < 4:
             gather(s + 1)
@@ -313,11 +315,22 @@
             for part in range(2)
         ]
         made.at[s].reshape(512, MW)[...] = dot(behind[...], jnp.concatenate(scaled, 0)).astype(BF)
-        send = pltpu.make_async_copy(made.at[s], out.at[pl.ds(s * 256, 256)], sems_out.at[s])
         send.start()
-        sends.append(send)
         if s < 4:
             project(s + 1)
+
+    for group in ((0, 1), (2, 3), (4,)):
+        leaving = [
+            pltpu.make_async_copy(made.at[s], out.at[pl.ds(s * 256, 256)], sems_out.at[s])
+            for s in group
+        ]
+
+        @pl.when(waves[0] >= 0)
+        def _(group=group, leaving=leaving):
+            for s, send in zip(group, leaving):
+                work(s, send)
+
+        sends.extend(leaving)
     for send in sends:
         send.wait()
 

time: 83.4 us -> 83 us (level)
  Pallas kernels: 25.1 us -> 24 us
  transfers between devices with their start and end apart: 5 -> 5, of which waited for: 3 -> 3; matrix products, arithmetic and copies ran while one was open for 0% -> 0% of each run, Pallas kernels for 8% -> 7%
where the time goes in v4:
time: 83 us; the launch traced here: 82.7 us
  waiting for transfers between devices  32.2 us (39%)
  Pallas kernels  24 us (29%)
  starting transfers between devices  20.7 us (25%)
  local copies, waits for them, and re-layouts  4.97 us (6%)
  between operations  0.94 us (1%)
    all_to_all x1, waiting for transfers between devices, shards(): lax.all_to_all(fourier.reshape(256, 5, 4, BLK), ('lev', 'wave'), split_ax...  29.4 us
    ppermute x4, starting transfers between devices, shards(): came.append(lax.ppermute(message, 'wave', route))  11.3 us
    pallas_call x1, Pallas kernels, receive(): pl.pallas_call(receive_kernel, out_shape=jax.ShapeDtypeStruct((5 * 256, 2...  10.2 us
    all_to_all x1, starting transfers between devices, shards(): lax.all_to_all(fourier.reshape(256, 5, 4, BLK), ('lev', 'wave'), split_ax...  9.36 us
    pallas_call x1, Pallas kernels, dft(): pl.pallas_call(dft_kernel, out_shape=jax.ShapeDtypeStruct((MW * 4, BLK),...  6.12 us
    unnamed x16, local copies, waits for them, and re-layouts  4.97 us
    pallas_call x1, Pallas kernels, prepare(): pl.pallas_call(prepare_kernel, out_shape=[jax.ShapeDtypeStruct((256, 256)...  3.64 us
    ppermute x4, waiting for transfers between devices, shards(): came.append(lax.ppermute(message, 'wave', route))  2.73 us
  transfers between devices with their start and end apart: 5, of which 3 were waited for; matrix products, arithmetic and copies ran while one was open for 0% of the time, Pallas kernels for 7%

profile of v4, /device:TPU:1, one launch (start us, length us, event | category | flops | bytes accessed | tf_op | source)
XLA Modules:
  0.0 82.7 jit_solution(15453757349535986572)
XLA Ops:
  0.0 0.0 copy-start.4
  0.7 1.9 %pack.1 = (bf16[272,128]{1,0:T(8,128)(2,1)}, bf16[272,128]{1,0:T(8,128)(2,1)}, bf16[272,128]{1,0:T(8,128)(2,1)}, bf16[272,128]{1,0:T(8,128)(2,1)}) custom-call(s32[1,32]{1,0:T(1,128)} %owner.1, s32[1,32]{1,0:T(1,128)} %block.1, s32[1]{0:T(128)S(6)} %copy.13.count, f32[32,32,128]{2,1,0:T(8,128)} %bitcast.11), custom_call_target="tpu_custom_call" | custom-call | bytes 1048576 | tf_op jit(solution)/shard_map/pack/pallas_call | solution.py:94
  2.5 9.1 %collective-permute-start = (bf16[272,128]{1,0:T(8,128)(2,1)}, bf16[272,128]{1,0:T(8,128)(2,1)S(1)}, u32[]{:S(2)}, u32[]{:S(2)}) collective-permute-start(bf16[272,128]{1,0:T(8,128)(2,1)} %get-tuple-element.17), channel_id=1, source_target_pairs={{0,30},{1,31},{2,0},{3,1},{4,2},{5,3},{6,4},{7,5},{8,6},{9,7},{10,... | collective-permute-start | bytes 208904 | tf_op jit(solution)/shard_map/ppermute | solution.py:370
  11.7 0.8 collective-permute-start.1
  12.4 0.7 collective-permute-start.2
  13.1 0.7 collective-permute-start.3
  13.8 0.0 copy-start
  13.8 1.4 %copy-done = bf16[8,4,8,2816]{3,2,1,0:T(8,128)(2,1)S(1)} copy-done((bf16[8,4,8,2816]{3,2,1,0:T(8,128)(2,1)S(1)}, bf16[8,4,8,2816]{3,2,1,0:T(8,128)(2,1)}, u32[]{:S(2)}) %copy-start) | copy-done | bytes 1441816
  15.2 0.0 copy-start.6
  15.2 2.2 %ready.1 = (bf16[22,256,128]{2,1,0:T(8,128)(2,1)S(1)}, bf16[1280,1408]{1,0:T(8,128)(2,1)S(1)}) custom-call(bf16[32,8,2816]{2,1,0:T(8,128)(2,1)S(1)} %bitcast.7, bf16[1280,1408]{1,0:T(8,128)(2,1)} %constant.4.clone.table), custom_call_target="tpu_custom_call" | custom-call | bytes 10485760 | tf_op jit(solution)/shard_map/ready/pallas_call | solution.py:128
  17.4 0.0 collective-permute-done.m0
  17.4 0.0 collective-permute-done.1.m1
  17.4 1.7 %collective-permute-done.2.m2 = bf16[272,128]{1,0:T(8,128)(2,1)S(1)} collective-permute-done((bf16[272,128]{1,0:T(8,128)(2,1)}, bf16[272,128]{1,0:T(8,128)(2,1)S(1)}, u32[]{:S(2)}, u32[]{:S(2)}) %collective-permute-start.2) | collective-permute-done | bytes 69664 | tf_op jit(solution)/shard_map/ppermute | solution.py:370
  19.1 1.0 %collective-permute-done.3.m3 = bf16[272,128]{1,0:T(8,128)(2,1)S(1)} collective-permute-done((bf16[272,128]{1,0:T(8,128)(2,1)}, bf16[272,128]{1,0:T(8,128)(2,1)S(1)}, u32[]{:S(2)}, u32[]{:S(2)}) %collective-permute-start.3) | collective-permute-done | bytes 69664 | tf_op jit(solution)/shard_map/ppermute | solution.py:370
  20.1 0.0 copy-done.4
  20.1 0.0 copy-done.6
  20.1 0.0 copy-start.2
  20.1 0.0 copy-start.3
  20.2 0.0 copy-start.5
  20.2 6.1 %dft.1 = bf16[5120,128]{1,0:T(8,128)(2,1)} custom-call(bf16[272,128]{1,0:T(8,128)(2,1)S(1)} %collective-permute-done.m0, bf16[272,128]{1,0:T(8,128)(2,1)S(1)} %collective-permute-done.1.m1, bf16[272,128]{1,0:T(8,128)(2,1)S(1)} %collective-permute-done.2.m2, bf16[272,128]{1,0:T(8,128)(2,1)S(1)} %collective-permute-done.3.m3, s32[10,128]{1,0:T(8,128)S(1)} %bitcast.9, ...), custom_call_target="tpu_custom_call" | custom-call | flops 4294967296 | bytes 16777216 | tf_op jit(solution)/shard_map/dft/pallas_call | solution.py:198
  26.3 9.4 %all-to-all-start = ((bf16[256,5,4,128]{3,2,1,0:T(4,128)(2,1)}), bf16[256,5,4,128]{3,2,1,0:T(4,128)(2,1)S(1)}, u32[]{:S(2)}, u32[]{:S(2)}) async-start(bf16[256,5,4,128]{3,2,1,0:T(4,128)(2,1)} %bitcast.3), calls=%async_computation | async-start | bytes 2621440 | tf_op jit(solution)/shard_map/all_to_all | solution.py:374
  35.7 0.0 copy-done.2
  35.7 0.0 copy-done.3
  35.7 0.0 copy-done.5
  35.7 0.0 copy-start.1
  35.7 1.9 %copy-done.1 = bf16[5,256,1280]{2,1,0:T(8,128)(2,1)S(1)} copy-done((bf16[5,256,1280]{2,1,0:T(8,128)(2,1)S(1)}, bf16[5,256,1280]{2,1,0:T(8,128)(2,1)}, u32[]{:S(2)}) %copy-start.1) | copy-done | bytes 3276824
  37.6 3.6 %prepare.1 = (bf16[256,256]{1,0:T(8,128)(2,1)S(1)}, bf16[512,512]{1,0:T(8,128)(2,1)S(1)}, f32[256,1280]{1,0:T(8,128)S(1)}, bf16[5,256,1280]{2,1,0:T(8,128)(2,1)S(1)}) custom-call(f32[64,64]{1,0:T(8,128)S(1)} %copy-done.2, f32[64,64]{1,0:T(8,128)S(1)} %copy-done.3, f32[1,64]{1,0:T(1,128)S(1)} %bitcast.10, bf16[5,256,1280]{2,1,0:T(8,128)(2,1)S(1)} %copy-done.1), custom_call_target="tpu_custom_call" | custom-call | flops 2147483648 | bytes 8388608 | tf_op jit(solution)/shard_map/prepare/pallas_call | solution.py:257
  41.3 0.0 copy-start.7
  41.3 1.7 %copy-done.7 = bf16[5,256,1280]{2,1,0:T(8,128)(2,1)} copy-done((bf16[5,256,1280]{2,1,0:T(8,128)(2,1)}, bf16[5,256,1280]{2,1,0:T(8,128)(2,1)S(1)}, u32[]{:S(2)}) %copy-start.7) | copy-done | bytes 3276824
  42.9 29.4 %all-to-all-done = bf16[256,5,4,128]{3,2,1,0:T(4,128)(2,1)S(1)} async-done(((bf16[256,5,4,128]{3,2,1,0:T(4,128)(2,1)}), bf16[256,5,4,128]{3,2,1,0:T(4,128)(2,1)S(1)}, u32[]{:S(2)}, u32[]{:S(2)}) %all-to-all-start) | async-done | bytes 1310752 | tf_op jit(solution)/shard_map/all_to_all | solution.py:374
  72.4 10.2 %receive.1 = bf16[1280,2,1280]{2,1,0:T(2,128)(2,1)} custom-call(s32[1280]{0:T(1024)S(1)} %copy-done.4, bf16[5120,128]{1,0:T(8,128)(2,1)S(1)} %bitcast.8, bf16[5,256,1280]{2,1,0:T(8,128)(2,1)} %copy-done.7, bf16[256,256]{1,0:T(8,128)(2,1)S(1)} %get-tuple-element.26.ahead, bf16[512,512]{1,0:T(8,128)(2,1)S(1)} %get-tuple-element.27.behind, ...), custom_call_target="tpu_custom_call" | custom-call | flops 6442450944 | bytes 14680064 | tf_op jit(solution)/shard_map/receive/pallas_call | solution.py:340
Async XLA Ops:
  0.0 20.1 %copy-start.4 = (s32[1280]{0:T(1024)S(1)}, s32[1280]{0:T(1024)}, u32[]{:S(2)}) copy-start(s32[1280]{0:T(1024)} %waves.1) | copy-start | bytes 15364
  2.5 14.9 %collective-permute-start = (bf16[272,128]{1,0:T(8,128)(2,1)}, bf16[272,128]{1,0:T(8,128)(2,1)S(1)}, u32[]{:S(2)}, u32[]{:S(2)}) collective-permute-start(bf16[272,128]{1,0:T(8,128)(2,1)} %get-tuple-element.17), channel_id=1, source_target_pairs={{0,30},{1,31},{2,0},{3,1},{4,2},{5,3},{6,4},{7,5},{8,6},{9,7},{10,... | collective-permute-start | bytes 208904 | tf_op jit(solution)/shard_map/ppermute | solution.py:370
  11.7 5.8 %collective-permute-start.1 = (bf16[272,128]{1,0:T(8,128)(2,1)}, bf16[272,128]{1,0:T(8,128)(2,1)S(1)}, u32[]{:S(2)}, u32[]{:S(2)}) collective-permute-start(bf16[272,128]{1,0:T(8,128)(2,1)} %get-tuple-element.18), channel_id=1, source_target_pairs={{0,31},{1,0},{2,1},{3,2},{4,3},{5,4},{6,5},{7,6},{8,7},{9,8},{10,9... | collective-permute-start | bytes 208904 | tf_op jit(solution)/shard_map/ppermute | solution.py:370
  12.4 6.7 %collective-permute-start.2 = (bf16[272,128]{1,0:T(8,128)(2,1)}, bf16[272,128]{1,0:T(8,128)(2,1)S(1)}, u32[]{:S(2)}, u32[]{:S(2)}) collective-permute-start(bf16[272,128]{1,0:T(8,128)(2,1)} %get-tuple-element.19), channel_id=1, source_target_pairs={{0,1},{1,2},{2,3},{3,4},{4,5},{5,6},{6,7},{7,8},{8,9},{9,10},{10,1... | collective-permute-start | bytes 208904 | tf_op jit(solution)/shard_map/ppermute | solution.py:370
  13.1 7.0 %collective-permute-start.3 = (bf16[272,128]{1,0:T(8,128)(2,1)}, bf16[272,128]{1,0:T(8,128)(2,1)S(1)}, u32[]{:S(2)}, u32[]{:S(2)}) collective-permute-start(bf16[272,128]{1,0:T(8,128)(2,1)} %get-tuple-element.20), channel_id=1, source_target_pairs={{0,2},{1,3},{2,4},{3,5},{4,6},{5,7},{6,8},{7,9},{8,10},{9,11},{10,... | collective-permute-start | bytes 208904 | tf_op jit(solution)/shard_map/ppermute | solution.py:370
  13.8 1.4 %copy-start = (bf16[8,4,8,2816]{3,2,1,0:T(8,128)(2,1)S(1)}, bf16[8,4,8,2816]{3,2,1,0:T(8,128)(2,1)}, u32[]{:S(2)}) copy-start(bf16[8,4,8,2816]{3,2,1,0:T(8,128)(2,1)} %param.12) | copy-start | bytes 4325380
  15.2 4.9 %copy-start.6 = (bf16[1280,1408]{1,0:T(8,128)(2,1)S(1)}, bf16[1280,1408]{1,0:T(8,128)(2,1)}, u32[]{:S(2)}) copy-start(bf16[1280,1408]{1,0:T(8,128)(2,1)} %constant.5.clone.odd) | copy-start | bytes 10813444
  20.1 15.5 %copy-start.2 = (f32[64,64]{1,0:T(8,128)S(1)}, f32[64,64]{1,0:T(8,128)}, u32[]{:S(2)}) copy-start(f32[64,64]{1,0:T(8,128)} %modes.1) | copy-start | bytes 49156
  20.1 15.5 %copy-start.3 = (f32[64,64]{1,0:T(8,128)S(1)}, f32[64,64]{1,0:T(8,128)}, u32[]{:S(2)}) copy-start(f32[64,64]{1,0:T(8,128)} %back.1) | copy-start | bytes 49156
  20.2 15.5 %copy-start.5 = (f32[64]{0:T(128)S(1)}, f32[64]{0:T(128)}, u32[]{:S(2)}) copy-start(f32[64]{0:T(128)} %param.21) | copy-start | bytes 772
  26.3 46.1 %all-to-all-start = ((bf16[256,5,4,128]{3,2,1,0:T(4,128)(2,1)}), bf16[256,5,4,128]{3,2,1,0:T(4,128)(2,1)S(1)}, u32[]{:S(2)}, u32[]{:S(2)}) async-start(bf16[256,5,4,128]{3,2,1,0:T(4,128)(2,1)} %bitcast.3), calls=%async_computation | async-start | bytes 2621440 | tf_op jit(solution)/shard_map/all_to_all | solution.py:374
  35.7 1.9 %copy-start.1 = (bf16[5,256,1280]{2,1,0:T(8,128)(2,1)S(1)}, bf16[5,256,1280]{2,1,0:T(8,128)(2,1)}, u32[]{:S(2)}) copy-start(bf16[5,256,1280]{2,1,0:T(8,128)(2,1)} %legendre) | copy-start | bytes 9830404
  41.3 1.7 %copy-start.7 = (bf16[5,256,1280]{2,1,0:T(8,128)(2,1)}, bf16[5,256,1280]{2,1,0:T(8,128)(2,1)S(1)}, u32[]{:S(2)}) copy-start(bf16[5,256,1280]{2,1,0:T(8,128)(2,1)S(1)} %get-tuple-element.25.legendre) | copy-start | bytes 9830404
